TPU v7x, 128 devices: a whole 4x4x4 slice. The times are simulated.
128 devices in a mesh: dom: 4 (over x), head: 32 (over z, y, core).
Axes of the slice: x: 4, y: 4, z: 4, core: 2. Of those that a mesh axis runs over, the one named last changes fastest.
Arguments:
- tokens: bfloat16 [24, 64, 8192], P(None, 'dom', 'head'), may hold values from -6 to 6
- parents: int32 [64], replicated, may hold values from 0 to 63, as said below
- recurrent_state: float32 [64, 128, 64, 256], P('dom', 'head'), may hold values from -6 to 6
- value_history: float32 [64, 3, 8192], P('dom', None, 'head'), may hold values from -6 to 6
- mixing_history: float32 [64, 3, 2048], P('dom', None, 'head'), may hold values from -6 to 6
- input_gain: float32 [8192], P('head'), may hold values from 0.5 to 1.5
- gate_value_weight: bfloat16 [8192, 2, 8192], P(None, None, 'head'), may hold values from -0.0625 to 0.0625
- mixing_weight: bfloat16 [8192, 2048], P(None, 'head'), may hold values from -0.0625 to 0.0625
- step_weight: bfloat16 [8192, 128], P(None, 'head'), may hold values from -0.0625 to 0.0625
- value_kernel: float32 [4, 8192], P(None, 'head'), may hold values from -3 to 3
- value_offset: float32 [8192], P('head'), may hold values from -0.5 to 0.5
- mixing_kernel: float32 [4, 2048], P(None, 'head'), may hold values from -3 to 3
- mixing_offset: float32 [2048], P('head'), may hold values from -0.5 to 0.5
- step_offset: float32 [128], P('head'), may hold values from -4 to 0
- decay_log: float32 [128], P('head'), may hold values from -2 to 1.5
- skip_gain: float32 [128], P('head'), may hold values from 0.5 to 1.5
- output_gain: float32 [8192], P('head'), may hold values from 0.5 to 1.5
- output_weight: bfloat16 [8192, 8192], P('head'), may hold values from -0.0625 to 0.0625
Outputs:
- mixed: bfloat16 [24, 64, 8192], P(None, 'dom', 'head')
Inputs may be any that keep to these rules, and one draw needn't show every extreme that they name: parents comes from systematic resampling: it never falls with i, and offspring counts are very uneven, so that a particle's parent may sit several blocks of 16 particles away.
All inputs are finite; a program needn't handle non-finite values.
Results may differ from a plain program's by a relative error of at most 0.023.
Values may be sent and summed in bfloat16 or wider, within the bound.
A program may use at most 128 MiB of HBM per device.

v0:
```python
import jax
import jax.numpy as jnp
from jax import lax
from jax.sharding import PartitionSpec as P

HEADS = 128
GROUPS = 4
P_SIZE = 64


def causal_conv(previous, current, kernel, shift_bias):
    window = jnp.concatenate([jnp.moveaxis(previous, 1, 0), current], axis=0)
    length = current.shape[0]
    summed = jnp.zeros_like(current)
    for tap_index in range(kernel.shape[0]):
        summed = summed + kernel[tap_index] * window[tap_index : tap_index + length]
    return jax.nn.silu(summed + shift_bias)


def pick_rows(carried, pieces, wanted):
    counted = pieces[0].shape[0]
    inside = (wanted >= 0) & (wanted < counted)
    safe_rows = jnp.clip(wanted, 0, counted - 1)
    result = []
    for held_rows, source in zip(carried, pieces):
        taken_rows = jnp.take(source, safe_rows, axis=0)
        mask_shape = (wanted.shape[0],) + (1,) * (source.ndim - 1)
        result.append(jnp.where(inside.reshape(mask_shape), taken_rows, held_rows))
    return tuple(result)


def body(
    tokens,
    parents,
    recurrent_state,
    value_history,
    mixing_history,
    input_gain,
    gate_value_weight,
    mixing_weight,
    step_weight,
    value_kernel,
    value_offset,
    mixing_kernel,
    mixing_offset,
    step_offset,
    decay_log,
    skip_gain,
    output_gain,
    output_weight,
):
    steps_count, local_particles, local_width = tokens.shape
    local_heads, head_width, state_width = (
        recurrent_state.shape[1],
        recurrent_state.shape[2],
        recurrent_state.shape[3],
    )
    channels = local_heads * head_width
    row_count = steps_count * local_particles
    dom_index = lax.axis_index("dom")
    head_count = lax.axis_size("head")
    head_index = lax.axis_index("head")
    gathered, full_gain = (
        lax.all_gather(tokens, "head", axis=2, tiled=True),
        lax.all_gather(input_gain.astype(jnp.bfloat16), "head", axis=0, tiled=True).astype(
            input_gain.dtype
        ),
    )
    flat_tokens = gathered.astype(jnp.float32).reshape(row_count, -1)
    normed = (
        flat_tokens
        * lax.rsqrt(jnp.mean(flat_tokens * flat_tokens, axis=-1, keepdims=True) + 1e-05)
        * full_gain
    ).astype(jnp.bfloat16)
    gate_value = jnp.dot(
        normed,
        gate_value_weight.reshape(gate_value_weight.shape[0], 2 * channels),
        preferred_element_type=jnp.float32,
    ).reshape(steps_count, local_particles, 2, channels)
    mixing_raw = jnp.dot(normed, mixing_weight, preferred_element_type=jnp.float32).reshape(
        steps_count, local_particles, -1
    )
    step_raw = jnp.dot(normed, step_weight, preferred_element_type=jnp.float32).reshape(
        steps_count, local_particles, local_heads
    )
    first_child = dom_index * local_particles
    own_parents = lax.dynamic_slice_in_dim(parents, first_child, local_particles)
    initial = (
        jnp.zeros_like(recurrent_state),
        jnp.zeros_like(value_history),
        jnp.zeros_like(mixing_history),
    )
    start_state, value_prev, mixing_prev = pick_rows(
        initial,
        (
            lax.all_gather(recurrent_state.astype(jnp.bfloat16), "dom", axis=0, tiled=True).astype(
                jnp.float32
            ),
            lax.all_gather(value_history.astype(jnp.bfloat16), "dom", axis=0, tiled=True).astype(
                jnp.float32
            ),
            lax.all_gather(mixing_history.astype(jnp.bfloat16), "dom", axis=0, tiled=True).astype(
                jnp.float32
            ),
        ),
        own_parents,
    )
    value_act = causal_conv(value_prev, gate_value[:, :, 1], value_kernel, value_offset).reshape(
        steps_count, local_particles, local_heads, head_width
    )
    mixing_act = causal_conv(mixing_prev, mixing_raw, mixing_kernel, mixing_offset)
    mixing_all = lax.all_gather(mixing_act.astype(jnp.bfloat16), "head", axis=2, tiled=True).astype(
        mixing_act.dtype
    )
    per_group = head_count // GROUPS
    group_index = head_index // per_group
    input_mix = lax.dynamic_slice_in_dim(mixing_all, group_index * state_width, state_width, 2)
    output_mix = lax.dynamic_slice_in_dim(
        mixing_all, (GROUPS + group_index) * state_width, state_width, 2
    )
    step_size = jax.nn.softplus(step_raw + step_offset)
    decay = jnp.exp(-step_size * jnp.exp(decay_log))
    skip_term = skip_gain[:, None] * value_act

    def advance(state_now, inputs):
        value_now, input_now, output_now, size_now, decay_now = inputs
        state_now = (
            decay_now[:, :, None, None] * state_now
            + (size_now[:, :, None] * value_now)[..., None] * input_now[:, None, None, :]
        )
        read_out = jnp.einsum(
            "bhpn,bn->bhp", state_now, output_now, precision=lax.Precision.HIGHEST
        )
        return (state_now, read_out)

    unused_state, local_read = lax.scan(
        advance, start_state, (value_act, input_mix, output_mix, step_size, decay)
    )
    read_all = local_read + skip_term
    gated = read_all * jax.nn.silu(
        gate_value[:, :, 0].reshape(steps_count, local_particles, local_heads, head_width)
    )
    squares = jnp.sum(gated * gated, axis=(2, 3))
    selector = jnp.arange(GROUPS, dtype=jnp.int32) == group_index
    slots = jnp.where(selector, squares[..., None], 0.0)
    summed = lax.psum(slots, "head")
    group_total = jnp.sum(jnp.where(selector, summed, 0.0), axis=-1)
    square_mean = group_total / (HEADS // GROUPS * P_SIZE)
    scaled = (
        (gated * lax.rsqrt(square_mean[..., None, None] + 1e-05)).reshape(row_count, channels)
        * output_gain
    ).astype(jnp.bfloat16)
    output_terms = jnp.dot(scaled, output_weight, preferred_element_type=jnp.float32).reshape(
        steps_count, local_particles, -1
    )
    return lax.psum_scatter(
        output_terms.astype(jnp.bfloat16), "head", scatter_dimension=2, tiled=True
    )


def solution(mesh):
    return jax.shard_map(
        body,
        mesh=mesh,
        in_specs=(
            P(None, "dom", "head"),
            P(),
            P("dom", "head", None, None),
            P("dom", None, "head"),
            P("dom", None, "head"),
            P("head"),
            P(None, None, "head"),
            P(None, "head"),
            P(None, "head"),
            P(None, "head"),
            P("head"),
            P(None, "head"),
            P("head"),
            P("head"),
            P("head"),
            P("head"),
            P("head"),
            P("head", None),
        ),
        out_specs=P(None, "dom", "head"),
        check_vma=False,
    )
```

profile of v0, /device:TPU:0, one launch (start us, length us, event | category | flops | bytes accessed | tf_op | source)
XLA Modules:
  0.0 750.3 jit_solution(15983251670227247696)
XLA Ops:
  11.3 8.1 %copy.52 = bf16[1024,8,2,256]{3,1,2,0:T(8,128)(2,1)} copy(bf16[1024,8,2,256]{3,2,1,0:T(2,128)(2,1)} %bitcast.78) | data formatting | bytes 16777216
  19.4 11.5 %copy.43 = bf16[512,8192]{1,0:T(8,128)(2,1)} copy(bf16[512,8192]{0,1:T(8,128)(2,1)} %bitcast.77) | data formatting | bytes 16777216 | tf_op jit(solution)/shard_map/dot_general | solution.py:75
  30.9 25.8 %all-gather = bf16[32,1,256]{2,1,0:T(2,128)(2,1)S(1)} all-gather(bf16[1,1,256]{2,1,0:T(2,128)(2,1)S(1)} %reshape.138), channel_id=1, replica_groups=mesh['dom'=4,'head'=32] {'head'}, dimensions={0}, use_global_device_ids=true | all-gather | bytes 16896 | tf_op jit(solution)/shard_map/all_gather | solution.py:65
  56.8 12.3 %all_gather.21 = bf16[64,3,256]{2,0,1:T(8,128)(2,1)S(1)} all-gather(bf16[16,3,256]{2,0,1:T(8,128)(2,1)S(1)} %convert_element_type.52), channel_id=1, replica_groups=mesh['dom'=4,'head'=32] {'dom'}, dimensions={0}, use_global_device_ids=true | all-gather | bytes 122880 | tf_op jit(solution)/shard_map/all_gather | solution.py:99
  69.2 11.9 %all_gather.22 = bf16[64,3,64]{2,0,1:T(8,128)(2,1)S(1)} all-gather(bf16[16,3,64]{2,0,1:T(8,128)(2,1)S(1)} %convert_element_type.54), channel_id=1, replica_groups=mesh['dom'=4,'head'=32] {'dom'}, dimensions={0}, use_global_device_ids=true | all-gather | bytes 30720 | tf_op jit(solution)/shard_map/all_gather | solution.py:102
  82.7 4.4 fusion.2
  90.7 7.9 %fusion.5 = f32[24,16,2,256]{3,1,2,0:T(8,128)S(1)} fusion(bf16[2,256,8192,1]{2,1,0,3:T(8,128)(2,1)} %bitcast.79, bf16[24,16,8192]{2,1,0:T(8,128)(2,1)} %all-gather.7.cloned.1.call-done, f32[8192]{0:T(1024)S(1)} %bitcast.82, f32[24,16]{1,0:T(8,128)S(1)} %add_rsqrt_fusion.1), kind=kOutput, calls=%fused_computation.18 | convolution fusion | flops 3233808384 | bytes 15500800 | tf_op jit(solution)/shard_map/dot_general | solution.py:75
  100.4 10.4 %multiply_exponential_fusion = (f32[24,16,4]{1,2,0:T(4,128)S(1)}, f32[24,16,4]{1,2,0:T(4,128)S(1)}) fusion(f32[4]{0:T(128)S(1)} %exp.23, f32[4]{0:T(128)S(1)} %copy-done.16, bf16[8192,4]{0,1:T(4,128)(2,1)S(1)} %copy-done.13, bf16[24,16,8192]{2,1,0:T(8,128)(2,1)} %all-gather.7.cloned.1.call-done, f32[8192]{0:T(1024)S(1)} %bitcast.83, ...), kind=kOutput, calls=%fused_computation.69 | convolution fusion | flops 37762560 | bytes 6403616 | tf_op jit(solution)/shard_map/dot_general | solution.py:83
  110.8 40.1 %all-gather.5.cloned.1.call-done = bf16[64,4,64,256]{3,2,1,0:T(8,128)(2,1)} async-done(((bf16[16,4,64,256]{3,2,1,0:T(8,128)(2,1)}), bf16[64,4,64,256]{3,2,1,0:T(8,128)(2,1)}) %all-gather.5.cloned.1.call-update) | async-done | bytes 8388624 | tf_op jit(solution)/shard_map/all_gather | solution.py:96
  150.9 11.3 %convert_element_type.47 = f32[64,4,64,256]{3,2,1,0:T(8,128)} convert(bf16[64,4,64,256]{3,2,1,0:T(8,128)(2,1)} %all-gather.5.cloned.1.call-done) | non-fusion elementwise | flops 4194304 | bytes 25165824 | tf_op jit(solution)/shard_map/convert_element_type | solution.py:96
  162.2 8.9 %gather_fusion = f32[16,4,64,256]{3,2,1,0:T(8,128)} fusion(f32[64,4,64,256]{3,2,1,0:T(8,128)} %convert_element_type.47, s32[1024]{0:T(1024)S(1)} %pad_clamp_fusion), kind=kCustom, calls=%fused_computation | custom fusion | bytes 8388672 | tf_op jit(solution)/shard_map/jit(_take)/gather | solution.py:26
  171.1 5.2 select_select_fusion
  176.3 30.9 %all-gather.9.cloned.1.call-done = bf16[24,16,2048]{0,1,2:T(8,128)(2,1)} async-done(((bf16[24,16,64]{0,1,2:T(8,128)(2,1)}), bf16[24,16,2048]{0,1,2:T(8,128)(2,1)}) %all-gather.9.cloned.1.call-update) | async-done | bytes 1572880 | tf_op jit(solution)/shard_map/all_gather | solution.py:112
  207.2 4.6 convert_element_type.57
  218.0 306.0 %while.12 = (s32[]{:T(128)}, f32[16,4,64,256]{3,2,1,0:T(8,128)}, f32[24,16,4,64]{3,2,1,0:T(4,128)}, f32[24,16,4]{1,2,0:T(4,128)S(1)}, f32[24,16,4]{1,2,0:T(4,128...) while((s32[]{:T(128)}, f32[16,4,64,256]{3,2,1,0:T(8,128)}, ...), condition=%wide.region_2.3_spmd, body=%wide.region_1.2_spmd.sunk | while | flops 15732738 | bytes 12798585 | solution.py:136
  223.0 7.2 fusion.55
  231.0 4.0 multiply_add_fusion.2
  235.7 7.2 fusion.55
  248.5 7.2 fusion.55
  256.5 4.0 multiply_add_fusion.2
  261.2 7.2 fusion.55
  274.0 7.2 fusion.55
  282.0 4.0 multiply_add_fusion.2
  286.7 7.2 fusion.55
  299.5 7.2 fusion.55
  312.2 7.2 fusion.55
  325.0 7.2 fusion.55
  333.0 4.0 multiply_add_fusion.2
  337.7 7.2 fusion.55
  350.5 7.2 fusion.55
  363.2 7.2 fusion.55
  371.3 4.0 multiply_add_fusion.2
  376.0 7.2 fusion.55
  384.0 4.0 multiply_add_fusion.2
  388.7 7.2 fusion.55
  401.5 7.2 fusion.55
  414.2 7.2 fusion.55
  427.0 7.2 fusion.55
  439.7 7.2 fusion.55
  452.5 7.2 fusion.55
  465.2 7.2 fusion.55
  478.0 7.2 fusion.55
  490.7 7.2 fusion.55
  503.5 7.2 fusion.55
  516.2 7.2 fusion.55
  526.6 126.5 %psum.7 = f32[24,16,4]{1,2,0:T(4,128)S(1)} all-reduce(f32[24,16,4]{1,2,0:T(4,128)S(1)} %broadcast_select_fusion), channel_id=1, replica_groups=mesh['dom'=4,'head'=32] {'head'}, use_global_device_ids=true, to_apply=%region_4.5 | all-reduce | flops 1536 | bytes 12288 | tf_op jit(solution)/shard_map/psum | solution.py:146
  654.2 6.7 convolution_convert_fusion
  661.0 82.8 %reduce-scatter.2.cloned.1.call-done = bf16[24,16,256]{2,1,0:T(8,128)(2,1)} async-done(((bf16[24,16,8192]{2,1,0:T(8,128)(2,1)}), bf16[24,16,256]{2,1,0:T(8,128)(2,1)}) %reduce-scatter.2.cloned.1.call-update) | async-done | bytes 196624 | tf_op jit(solution)/shard_map/reduce_scatter | solution.py:156
  (265 shorter events, 131.6 us)
Async XLA Ops:
  6.5 80.5 %copy-start = (bf16[8192,64]{0,1:T(8,128)(2,1)S(1)}, bf16[8192,64]{0,1:T(8,128)(2,1)}, u32[]{:S(2)}) copy-start(bf16[8192,64]{0,1:T(8,128)(2,1)} %param.27) | copy-start | bytes 3145732
  6.5 76.1 %all-gather.7.cloned.1.call-start = ((), (), s32[]{:S(2)}) async-start(), calls=%async_computation.2 | async-start | bytes 6488064 | tf_op jit(solution)/shard_map/all_gather | solution.py:64
  7.3 143.7 %all-gather.5.cloned.1.call-start = ((), (), s32[]{:S(2)}) async-start(), calls=%async_computation.1 | async-start | bytes 10485760 | tf_op jit(solution)/shard_map/all_gather | solution.py:96
  11.2 196.0 %all-gather.9.cloned.1.call-start = ((), (), s32[]{:S(2)}) async-start(), calls=%async_computation.3 | async-start | bytes 8650752 | tf_op jit(solution)/shard_map/all_gather | solution.py:112
  19.4 11.5 %copy-start.14 = (f32[256]{0:T(256)S(1)}, f32[256]{0:T(256)}, u32[]{:S(2)}) copy-start(f32[256]{0:T(256)} %param.25) | copy-start | bytes 3076
  19.4 37.4 %copy-start.15 = (f32[4]{0:T(128)S(1)}, f32[4]{0:T(128)}, u32[]{:S(2)}) copy-start(f32[4]{0:T(128)} %param.34) | copy-start | bytes 52
  19.4 37.4 %copy-start.4 = (f32[16,3,256]{2,0,1:T(8,128)S(1)}, f32[16,3,256]{2,0,1:T(8,128)}, u32[]{:S(2)}) copy-start(f32[16,3,256]{2,0,1:T(8,128)} %param.23) | copy-start | bytes 147460
  19.4 49.8 %copy-start.5 = (f32[16,3,64]{2,0,1:T(8,128)S(1)}, f32[16,3,64]{2,0,1:T(8,128)}, u32[]{:S(2)}) copy-start(f32[16,3,64]{2,0,1:T(8,128)} %param.24) | copy-start | bytes 36868
  19.4 61.8 %copy-start.11 = (s32[64]{0:T(128)S(1)}, s32[64]{0:T(128)}, u32[]{:S(2)}) copy-start(s32[64]{0:T(128)} %param.21) | copy-start | bytes 772
  19.4 63.1 %copy-start.8 = (f32[4,64]{1,0:T(4,128)S(1)}, f32[4,64]{1,0:T(4,128)}, u32[]{:S(2)}) copy-start(f32[4,64]{1,0:T(4,128)} %param.31) | copy-start | bytes 3076
  19.4 63.1 %copy-start.6 = (f32[4,256]{1,0:T(4,128)S(1)}, f32[4,256]{1,0:T(4,128)}, u32[]{:S(2)}) copy-start(f32[4,256]{1,0:T(4,128)} %param.29) | copy-start | bytes 12292
  82.7 4.8 copy-start.2
  87.4 1.9 copy-start.10
  90.4 653.4 %reduce-scatter.2.cloned.1.call-start = ((), (), s32[]{:S(2)}) async-start(), calls=%async_computation.4 | async-start | bytes 6488064 | tf_op jit(solution)/shard_map/reduce_scatter | solution.py:156
  90.6 9.3 %copy-start.9 = (f32[256]{0:T(256)S(1)}, f32[256]{0:T(256)}, u32[]{:S(2)}) copy-start(f32[256]{0:T(256)} %param.30) | copy-start | bytes 3076
  90.6 9.8 %copy-start.13 = (bf16[8192,4]{0,1:T(4,128)(2,1)S(1)}, bf16[8192,4]{0,1:T(4,128)(2,1)}, u32[]{:S(2)}) copy-start(bf16[8192,4]{0,1:T(4,128)(2,1)} %param.28) | copy-start | bytes 196612
  90.6 9.8 %copy-start.16 = (f32[4]{0:T(128)S(1)}, f32[4]{0:T(128)}, u32[]{:S(2)}) copy-start(f32[4]{0:T(128)} %param.33) | copy-start | bytes 52
  218.0 306.0 %copy-start.3 = (f32[24,16,4,64]{3,2,1,0:T(4,128)S(1)}, f32[24,16,4,64]{3,2,1,0:T(4,128)}, u32[]{:S(2)}) copy-start(f32[24,16,4,64]{3,2,1,0:T(4,128)} %reshape_squeeze.3) | copy-start | bytes 1179652
  218.0 306.0 %copy-start.12 = (f32[4]{0:T(128)S(1)}, f32[4]{0:T(128)}, u32[]{:S(2)}) copy-start(f32[4]{0:T(128)} %param.35) | copy-start | bytes 52
  218.0 436.2 %copy-start.7 = (f32[256]{0:T(256)S(1)}, f32[256]{0:T(256)}, u32[]{:S(2)}) copy-start(f32[256]{0:T(256)} %param.36) | copy-start | bytes 3076
  654.2 89.6 %copy-start.1 = (bf16[8192,64]{0,1:T(8,128)(2,1)S(1)}, bf16[8192,64]{0,1:T(8,128)(2,1)}, u32[]{:S(2)}) copy-start(bf16[8192,64]{0,1:T(8,128)(2,1)} %param.27) | copy-start | bytes 3145732
Sparse Core Ops, SparseCore 0:
  9.5 57.0 all-gather.6
  68.3 82.6 all-gather.4
  153.2 53.9 all-gather.8
  661.1 82.6 reduce-scatter.1
where the time goes:
time: 753 us; the launch traced here: 750 us
  matrix products  199 us (26%)
  blocking collectives  177 us (24%)
  waiting for transfers between devices  155 us (21%)
  other arithmetic  131 us (17%)
  local copies, waits for them, and re-layouts  75.8 us (10%)
  between operations  13.5 us (2%)
    dot_general x24, matrix products, advance(): jnp.einsum('bhpn,bn->bhp', state_now, output_now, precision=lax.Precision...  172 us
    psum x1, blocking collectives, body(): summed = lax.psum(slots, 'head')  127 us
    add x24, other arithmetic, advance(): decay_now[:, :, None, None] * state_now  95.7 us
    reduce_scatter x1, waiting for transfers between devices, body(): lax.psum_scatter(output_terms.astype(jnp.bfloat16), 'head', scatter_dimen...  82.8 us
    all_gather x1, waiting for transfers between devices, body(): lax.all_gather(recurrent_state.astype(jnp.bfloat16), 'dom', axis=0, tiled...  40.1 us
    all_gather x1, waiting for transfers between devices, body(): lax.all_gather(mixing_act.astype(jnp.bfloat16), 'head', axis=2, tiled=True)  30.9 us
    all_gather x1, blocking collectives, body(): lax.all_gather(input_gain.astype(jnp.bfloat16), 'head', axis=0, tiled=True)  25.8 us
    squeeze x24, local copies, waits for them, and re-layouts, body(): lax.scan(advance, start_state, (value_act, input_mix, output_mix, step_si...  17.2 us
  transfers between devices with their start and end apart: 4, of which 3 were waited for; matrix products, arithmetic and copies ran while one was open for 10% of the time, Pallas kernels for 0%

commit v1 on v0

v1 whole, which is shorter than its diff:
```python
import jax
import jax.numpy as jnp
from jax import lax
from jax.sharding import PartitionSpec as P

STEPS = 24
LP = 16
ROWS = STEPS * LP
GROUPS = 4
LANES = 256
F32 = jnp.float32
BF16 = jnp.bfloat16


def silu(v):
    return v / (1.0 + jnp.exp(-v))


def conv_rows(window, kernel, bias):
    total = bias
    for k in range(4):
        total = total + kernel[k : k + 1] * window[k * LP : k * LP + ROWS]
    return silu(total)


def picked(hot, hist):
    return [jnp.dot(hot, hist[j], preferred_element_type=F32) for j in range(3)]


def body(
    tokens,
    parents,
    state,
    vhist,
    mhist,
    gain,
    gvw,
    mw,
    sw,
    vk,
    vo,
    mk,
    mo,
    so,
    dlog,
    skip,
    ogain,
    ow,
):
    d = lax.axis_index("dom")
    g = lax.axis_index("head") // 8
    full = lax.all_gather(tokens.reshape(ROWS, LANES), "head", axis=1, tiled=True)
    fgain = lax.all_gather(gain.astype(BF16), "head", axis=0, tiled=True).astype(F32)
    xf = full.astype(F32)
    inv = lax.rsqrt(jnp.mean(xf * xf, axis=-1, keepdims=True) + 1e-5)
    normed = (xf * inv * fgain).astype(BF16)
    gate = jnp.dot(normed, gvw[:, 0, :], preferred_element_type=F32)
    value = jnp.dot(normed, gvw[:, 1, :], preferred_element_type=F32)
    mixing = jnp.dot(normed, mw, preferred_element_type=F32)
    step_in = jnp.dot(normed, sw, preferred_element_type=F32)

    own = lax.dynamic_slice_in_dim(parents, d * LP, LP)
    hot = (own[:, None] == jnp.arange(64)[None, :]).astype(BF16)
    vall = lax.all_gather(
        jnp.moveaxis(vhist, 1, 0).astype(BF16), "dom", axis=1, tiled=True
    )
    mall = lax.all_gather(
        jnp.moveaxis(mhist, 1, 0).astype(BF16), "dom", axis=1, tiled=True
    )
    vact = conv_rows(jnp.concatenate(picked(hot, vall) + [value], 0), vk, vo[None])
    mact = conv_rows(jnp.concatenate(picked(hot, mall) + [mixing], 0), mk, mo[None])
    mixall = lax.all_gather(mact.astype(BF16), "head", axis=1, tiled=True)
    b = lax.dynamic_slice_in_dim(mixall, g * 256, 256, 1)
    c = lax.dynamic_slice_in_dim(mixall, (GROUPS + g) * 256, 256, 1)
    call = lax.all_gather(c, "dom", axis=0, tiled=False)

    sb = state.astype(BF16).reshape(LP, LANES, 256)
    row_parent = jnp.tile(parents.reshape(4, 1, LP), (1, STEPS, 1)).reshape(4 * ROWS)
    lhs = call.reshape(4 * ROWS, 256)
    u = jnp.zeros((4 * ROWS, LANES), F32)
    for q in range(LP):
        mask = (row_parent == d * LP + q).astype(BF16)[:, None]
        u = u + lax.dot_general(
            lhs * mask, sb[q], (((1,), (1,)), ((), ())), preferred_element_type=F32
        )
    from_state = lax.psum_scatter(
        u.astype(BF16).reshape(4, ROWS, LANES), "dom", scatter_dimension=0, tiled=True
    )[0].astype(F32)

    step = jax.nn.softplus(step_in + so[None])
    logdecay = -step * jnp.exp(dlog)[None]
    run = logdecay
    for sh in (1, 2, 4, 8, 16):
        z = jnp.zeros((sh * LP, 4), F32)
        run = run + jnp.concatenate([z, run[: ROWS - sh * LP]], 0)
    gram = lax.dot_general(c, b, (((1,), (1,)), ((), ())), preferred_element_type=F32)
    ri = lax.broadcasted_iota(jnp.int32, (ROWS, ROWS), 0)
    ci = lax.broadcasted_iota(jnp.int32, (ROWS, ROWS), 1)
    keep = ((ri % LP) == (ci % LP)) & (ci <= ri)
    gated = []
    for h in range(4):
        col = slice(64 * h, 64 * h + 64)
        diff = jnp.where(keep, run[:, h : h + 1] - run[:, h][None, :], -1e30)
        m = (gram * jnp.exp(diff)).astype(BF16)
        sv = (vact[:, col] * step[:, h : h + 1]).astype(BF16)
        y = jnp.dot(m, sv, preferred_element_type=F32)
        y = y + jnp.exp(run[:, h : h + 1]) * from_state[:, col]
        gated.append(y + skip[h] * vact[:, col])
    gated = jnp.concatenate(gated, 1) * silu(gate)
    sq = jnp.sum(gated * gated, axis=1)
    total = lax.psum(
        jnp.where(jnp.arange(GROUPS)[:, None] == g, sq[None, :], 0.0), "head"
    )
    total = jnp.sum(jnp.where(jnp.arange(GROUPS)[:, None] == g, total, 0.0), axis=0)
    inv2 = lax.rsqrt(total / 2048.0 + 1e-5)[:, None]
    scaled = (gated * inv2 * ogain[None]).astype(BF16)
    terms = jnp.dot(scaled, ow, preferred_element_type=F32).astype(BF16)
    out = lax.psum_scatter(terms, "head", scatter_dimension=1, tiled=True)
    return out.reshape(STEPS, LP, LANES)


def solution(mesh):
    return jax.shard_map(
        body,
        mesh=mesh,
        in_specs=(
            P(None, "dom", "head"),
            P(),
            P("dom", "head", None, None),
            P("dom", None, "head"),
            P("dom", None, "head"),
            P("head"),
            P(None, None, "head"),
            P(None, "head"),
            P(None, "head"),
            P(None, "head"),
            P("head"),
            P(None, "head"),
            P("head"),
            P("head"),
            P("head"),
            P("head"),
            P("head"),
            P("head", None),
        ),
        out_specs=P(None, "dom", "head"),
        check_vma=False,
    )
```

time: 753 us -> 367 us (0.49)
  matrix products: 199 us -> 43.2 us
  other arithmetic: 131 us -> 18 us
  blocking collectives: 177 us -> 132 us
  waiting for transfers between devices: 155 us -> 115 us
  local copies, waits for them, and re-layouts: 75.8 us -> 43.2 us
    dot_general x28 -> x32, matrix products: 199 us -> 43.2 us  [the longest x1 7.78 us: body(): value = jnp.dot(normed, gvw[:, 1, :], preferred_element_type=F32)]
    add x24 -> x5, other arithmetic: 95.7 us -> 0.24 us  [body(): run = run + jnp.concatenate([z, run[:ROWS - sh * LP]], 0)]
    psum x1, blocking collectives: 127 us -> 67.2 us  [body(): lax.psum(jnp.where(jnp.arange(GROUPS)[:, None] == g, sq[None, :], 0.0), '...]
    all_gather x3 -> x2, waiting for transfers between devices: 71 us -> 22.3 us  [the longest x1 22.3 us: body(): mixall = lax.all_gather(mact.astype(BF16), 'head', axis=1, tiled=True)]
    slice x1 -> x8, local copies, waits for them, and re-layouts: 0.01 us -> 20.1 us  [the longest x1 17.6 us: body(): gate = jnp.dot(normed, gvw[:, 0, :], preferred_element_type=F32)]
    squeeze x25 -> x0, local copies, waits for them, and re-layouts: 17.3 us -> none  [the longest x24 17.2 us: body(): lax.scan(advance, start_state, (value_act, input_mix, output_mix, step_si...]
    dynamic_update_slice x24 -> x0, local copies, waits for them, and re-layouts: 14.9 us -> none  [body(): lax.scan(advance, start_state, (value_act, input_mix, output_mix, step_si...]
    all_gather x3 -> x4, blocking collectives: 50 us -> 64.8 us  [the longest x1 25.7 us: body(): lax.all_gather(gain.astype(BF16), 'head', axis=0, tiled=True).astype(F32)]
  transfers between devices with their start and end apart: 4 -> 4, of which waited for: 3 -> 3; matrix products, arithmetic and copies ran while one was open for 10% -> 15% of each run, Pallas kernels for 0% -> 0%
where the time goes in v1:
time: 367 us; the launch traced here: 366 us
  blocking collectives  132 us (36%)
  waiting for transfers between devices  115 us (31%)
  local copies, waits for them, and re-layouts  43.2 us (12%)
  matrix products  43.2 us (12%)
  other arithmetic  18 us (5%)
  between operations  14.3 us (4%)
    reduce_scatter x1, waiting for transfers between devices, body(): out = lax.psum_scatter(terms, 'head', scatter_dimension=1, tiled=True)  81.4 us
    psum x1, blocking collectives, body(): lax.psum(jnp.where(jnp.arange(GROUPS)[:, None] == g, sq[None, :], 0.0), '...  67.2 us
    all_gather x1, blocking collectives, body(): lax.all_gather(gain.astype(BF16), 'head', axis=0, tiled=True).astype(F32)  25.7 us
    all_gather x1, waiting for transfers between devices, body(): mixall = lax.all_gather(mact.astype(BF16), 'head', axis=1, tiled=True)  22.3 us
    slice x1, local copies, waits for them, and re-layouts, body(): gate = jnp.dot(normed, gvw[:, 0, :], preferred_element_type=F32)  17.6 us
    all_gather x1, blocking collectives, body(): call = lax.all_gather(c, 'dom', axis=0, tiled=False)  14.9 us
    all_gather x1, blocking collectives, body(): lax.all_gather(jnp.moveaxis(mhist, 1, 0).astype(BF16), 'dom', axis=1, til...  12.2 us
    all_gather x1, blocking collectives, body(): lax.all_gather(jnp.moveaxis(vhist, 1, 0).astype(BF16), 'dom', axis=1, til...  11.9 us
  transfers between devices with their start and end apart: 4, of which 3 were waited for; matrix products, arithmetic and copies ran while one was open for 15% of the time, Pallas kernels for 0%

profile of v1, /device:TPU:0, one launch (start us, length us, event | category | flops | bytes accessed | tf_op | source)
XLA Modules:
  0.0 366.3 jit_solution(3251294010593405401)
XLA Ops:
  6.5 0.7 all-gather.5.cloned.1.call-update
  7.3 0.7 convert_element_type.297
  8.0 25.7 %all-gather.1 = bf16[32,1,256]{2,1,0:T(2,128)(2,1)S(1)} all-gather(bf16[1,1,256]{2,1,0:T(2,128)(2,1)S(1)} %reshape.451), channel_id=1, replica_groups=mesh['dom'=4,'head'=32] {'head'}, dimensions={0}, use_global_device_ids=true | all-gather | bytes 16896 | tf_op jit(solution)/shard_map/all_gather | solution.py:53
  34.4 0.7 dynamic_slice.9
  37.4 0.7 convert_element_type.338
  38.2 0.7 convert_element_type.335
  39.0 0.7 convert_element_type.332
  40.5 0.7 convert_element_type.326
  41.3 0.7 convert_element_type.323
  42.1 0.7 convert_element_type.320
  42.9 0.7 convert_element_type.317
  43.7 0.7 convert_element_type.314
  44.4 0.7 convert_element_type.311
  45.2 0.7 convert_element_type.307
  45.9 2.6 convert_element_type.308
  49.0 12.2 %all_gather.21 = bf16[3,64,64]{2,1,0:T(8,128)(2,1)S(1)} all-gather(bf16[3,16,64]{2,1,0:T(8,128)(2,1)S(1)} %convert_bitcast_fusion.1), channel_id=1, replica_groups=mesh['dom'=4,'head'=32] {'dom'}, dimensions={1}, use_global_device_ids=true | all-gather | bytes 30720 | tf_op jit(solution)/shard_map/all_gather | solution.py:67
  61.3 11.9 %all_gather.25 = bf16[3,64,256]{2,1,0:T(8,128)(2,1)S(1)} all-gather(bf16[3,16,256]{2,1,0:T(8,128)(2,1)S(1)} %convert_bitcast_fusion), channel_id=1, replica_groups=mesh['dom'=4,'head'=32] {'dom'}, dimensions={1}, use_global_device_ids=true | all-gather | bytes 122880 | tf_op jit(solution)/shard_map/all_gather | solution.py:64
  76.8 0.8 fusion.52
  77.6 0.8 fusion.53
  78.4 0.8 fusion.54
  79.2 0.9 fusion.49
  80.1 0.9 fusion.50
  81.0 0.9 fusion.51
  81.8 1.2 fusion.75
  83.0 4.3 %fusion = f32[384]{0:T(512)S(1)} fusion(bf16[384,8192]{1,0:T(8,128)(2,1)} %all-gather.5.cloned.1.call-done), kind=kLoop, calls=%fused_computation.2 | loop fusion | flops 9436800 | bytes 6292992 | tf_op jit(solution)/shard_map/reduce_sum | solution.py:55
  87.6 2.9 fusion.2
  90.6 2.1 fusion.78
  93.2 0.9 divide_convert_fusion
  94.2 17.6 %fusion.74 = (bf16[8192,1,256]{2,1,0:T(2,128)(2,1)}, bf16[8192,1,256]{2,1,0:T(2,128)(2,1)}) fusion(bf16[8192,2,256]{2,1,0:T(2,128)(2,1)} %param.24), kind=kLoop, calls=%fused_computation.198 | loop fusion | bytes 16777216 | tf_op jit(solution)/shard_map/slice | solution.py:57
  111.9 1.8 negate_multiply_fusion
  114.0 22.3 %all-gather.7.cloned.1.call-done = bf16[384,2048]{0,1:T(8,128)(2,1)} async-done(((bf16[384,64]{0,1:T(8,128)(2,1)}), bf16[384,2048]{0,1:T(8,128)(2,1)}) %all-gather.7.cloned.1.call-update) | async-done | bytes 1572880 | tf_op jit(solution)/shard_map/all_gather | solution.py:72
  136.3 0.9 constant_dynamic-slice_fusion
  137.2 14.9 %all-gather = bf16[1536,256]{0,1:T(8,128)(2,1)S(1)} all-gather(bf16[384,256]{0,1:T(8,128)(2,1)S(1)} %constant_dynamic-slice_fusion), channel_id=2, replica_groups=mesh['dom'=4,'head'=32] {'dom'}, dimensions={0}, use_global_device_ids=true | all-gather | bytes 983040 | tf_op jit(solution)/shard_map/all_gather | solution.py:75
  152.6 1.6 broadcast_multiply_fusion
  168.9 1.2 copy.74
  170.6 7.8 %fusion.4 = f32[384,256]{0,1:T(8,128)S(1)} fusion(bf16[384,8192]{1,0:T(8,128)(2,1)} %copy-done.2, bf16[8192,1,256]{2,1,0:T(2,128)(2,1)} %get-tuple-element.18), kind=kOutput, calls=%fused_computation.9 | convolution fusion | flops 1610612736 | bytes 10878976 | tf_op jit(solution)/shard_map/dot_general | solution.py:58
  178.5 0.8 add_divide_fusion
  179.2 1.2 fusion.32
  180.4 10.9 %reduce-scatter.3.cloned.1.call-done = bf16[1,384,256]{1,2,0:T(8,128)(2,1)} async-done(((bf16[4,384,256]{1,2,0:T(8,128)(2,1)}), bf16[1,384,256]{1,2,0:T(8,128)(2,1)}) %reduce-scatter.3.cloned.1.call-update) | async-done | bytes 196624 | tf_op jit(solution)/shard_map/reduce_scatter | solution.py:86
  191.3 1.0 bitcast_convert_fusion
  192.3 1.0 fusion.9
  193.3 1.1 fusion.8
  194.4 1.0 fusion.7
  195.5 1.1 fusion.6
  196.6 7.7 %multiply_reduce_fusion = (f32[384]{0:T(512)S(1)}, f32[384,256]{0,1:T(8,128)S(1)}) fusion(bf16[384,8192]{1,0:T(8,128)(2,1)} %copy-done.2, bf16[8192,1,256]{2,1,0:T(2,128)(2,1)} %get-tuple-element.17, f32[384,64]{0,1:T(8,128)S(1)} %fusion.6, f32[384,64]{0,1:T(8,128)S(1)} %fusion.7, f32[384,64]{0,1:T(8,128)S(1)} %fusion.8, f32[384,64]{0,1:T(8,128)S(1)} %fusion.9), kind=kOutput, calls=%fused_computation.57 | convolution fusion | flops 1611497088 | bytes 11273728 | tf_op jit(solution)/shard_map/dot_general | solution.py:57
  204.4 67.2 %psum.7 = f32[4,384]{1,0:T(4,128)S(1)} all-reduce(f32[4,384]{1,0:T(4,128)S(1)} %broadcast_select_fusion), channel_id=1, replica_groups=mesh['dom'=4,'head'=32] {'head'}, use_global_device_ids=true, to_apply=%region_3.4 | all-reduce | flops 1536 | bytes 12288 | tf_op jit(solution)/shard_map/psum | solution.py:111
  271.6 6.7 %convolution_convert_fusion = bf16[384,8192]{1,0:T(8,128)(2,1)} fusion(bf16[256,8192]{1,0:T(8,128)(2,1)} %param.35, f32[384,256]{0,1:T(8,128)S(1)} %get-tuple-element.82, f32[256]{0:T(256)S(1)} %copy-done.41, f32[384]{0:T(512)S(1)} %add_rsqrt_fusion), kind=kOutput, calls=%fused_computation.5 | convolution fusion | flops 1614053376 | bytes 10881536 | tf_op jit(solution)/shard_map/dot_general | solution.py:117
  278.4 81.4 %reduce-scatter.5.cloned.1.call-done = bf16[384,256]{1,0:T(8,128)(2,1)} async-done(((bf16[384,8192]{1,0:T(8,128)(2,1)}), bf16[384,256]{1,0:T(8,128)(2,1)}) %reduce-scatter.5.cloned.1.call-update) | async-done | bytes 196624 | tf_op jit(solution)/shard_map/reduce_scatter | solution.py:118
  (244 shorter events, 25.2 us)
Async XLA Ops:
  6.5 83.9 %copy-start = (bf16[8192,64]{0,1:T(8,128)(2,1)S(1)}, bf16[8192,64]{0,1:T(8,128)(2,1)}, u32[]{:S(2)}) copy-start(bf16[8192,64]{0,1:T(8,128)(2,1)} %param.25) | copy-start | bytes 3145732
  6.5 76.5 %all-gather.5.cloned.1.call-start = ((), (), s32[]{:S(2)}) async-start(), calls=%async_computation.2 | async-start | bytes 6488064 | tf_op jit(solution)/shard_map/all_gather | solution.py:52
  7.3 129.0 %all-gather.7.cloned.1.call-start = ((), (), s32[]{:S(2)}) async-start(), calls=%async_computation.3 | async-start | bytes 1622016 | tf_op jit(solution)/shard_map/all_gather | solution.py:72
  45.9 3.1 copy-start.28
  45.9 15.4 %copy-start.22 = (f32[16,3,256]{2,0,1:T(8,128)S(1)}, f32[16,3,256]{2,0,1:T(8,128)}, u32[]{:S(2)}) copy-start(f32[16,3,256]{2,0,1:T(8,128)} %param.21) | copy-start | bytes 147460
  45.9 29.0 %copy-start.42 = (f32[4]{0:T(128)S(1)}, f32[4]{0:T(128)}, u32[]{:S(2)}) copy-start(f32[4]{0:T(128)} %param.33) | copy-start | bytes 52
  45.9 29.7 %copy-start.55 = (f32[4,64]{1,0:T(4,128)S(1)}, f32[4,64]{1,0:T(4,128)}, u32[]{:S(2)}) copy-start(f32[4,64]{1,0:T(4,128)} %param.29) | copy-start | bytes 3076
  45.9 30.3 %copy-start.45 = (f32[4,256]{1,0:T(4,128)S(1)}, f32[4,256]{1,0:T(4,128)}, u32[]{:S(2)}) copy-start(f32[4,256]{1,0:T(4,128)} %param.27) | copy-start | bytes 12292
  83.0 4.6 %copy-start.4 = (bf16[384,8192]{1,0:T(8,128)(2,1)S(1)}, bf16[384,8192]{1,0:T(8,128)(2,1)}, u32[]{:S(2)}) copy-start(bf16[384,8192]{1,0:T(8,128)(2,1)} %all-gather.5.cloned.1.call-done) | copy-start | bytes 18874372
  90.5 2.7 copy-start.2
  90.5 2.7 copy-start.25
  90.5 2.7 copy-start.26
  90.5 2.7 copy-start.27
  90.5 2.7 copy-start.50
  90.5 2.7 copy-start.51
  94.1 17.7 %copy-start.21 = (bf16[8192,4]{0,1:T(4,128)(2,1)S(1)}, bf16[8192,4]{0,1:T(4,128)(2,1)}, u32[]{:S(2)}) copy-start(bf16[8192,4]{0,1:T(4,128)(2,1)} %param.26) | copy-start | bytes 196612
  94.1 17.7 %copy-start.43 = (f32[4]{0:T(128)S(1)}, f32[4]{0:T(128)}, u32[]{:S(2)}) copy-start(f32[4]{0:T(128)} %param.31) | copy-start | bytes 52
  94.1 17.7 %copy-start.44 = (f32[4]{0:T(128)S(1)}, f32[4]{0:T(128)}, u32[]{:S(2)}) copy-start(f32[4]{0:T(128)} %exp.42) | copy-start | bytes 52
  94.2 97.2 %reduce-scatter.3.cloned.1.call-start = ((), (), s32[]{:S(2)}) async-start(), calls=%async_computation.4 | async-start | bytes 983040 | tf_op jit(solution)/shard_map/reduce_scatter | solution.py:86
  94.2 17.7 %copy-start.3 = (bf16[384,8192]{1,0:T(8,128)(2,1)S(1)}, bf16[384,8192]{1,0:T(8,128)(2,1)}, u32[]{:S(2)}) copy-start(bf16[384,8192]{1,0:T(8,128)(2,1)} %copy-done.2) | copy-start | bytes 18874372
  113.6 38.7 %copy-start.29 = (bf16[4,384]{1,0:T(4,128)(2,1)S(1)}, bf16[4,384]{1,0:T(4,128)(2,1)}, u32[]{:S(2)}) copy-start(bf16[4,384]{1,0:T(4,128)(2,1)} %convert_element_type.341) | copy-start | bytes 9220
  113.7 38.7 %copy-start.30 = (bf16[4,384]{1,0:T(4,128)(2,1)S(1)}, bf16[4,384]{1,0:T(4,128)(2,1)}, u32[]{:S(2)}) copy-start(bf16[4,384]{1,0:T(4,128)(2,1)} %convert_element_type.338) | copy-start | bytes 9220
  113.7 38.7 %copy-start.31 = (bf16[4,384]{1,0:T(4,128)(2,1)S(1)}, bf16[4,384]{1,0:T(4,128)(2,1)}, u32[]{:S(2)}) copy-start(bf16[4,384]{1,0:T(4,128)(2,1)} %convert_element_type.335) | copy-start | bytes 9220
  113.7 38.8 %copy-start.32 = (bf16[4,384]{1,0:T(4,128)(2,1)S(1)}, bf16[4,384]{1,0:T(4,128)(2,1)}, u32[]{:S(2)}) copy-start(bf16[4,384]{1,0:T(4,128)(2,1)} %convert_element_type.332) | copy-start | bytes 9220
  113.7 38.8 %copy-start.33 = (bf16[4,384]{1,0:T(4,128)(2,1)S(1)}, bf16[4,384]{1,0:T(4,128)(2,1)}, u32[]{:S(2)}) copy-start(bf16[4,384]{1,0:T(4,128)(2,1)} %convert_element_type.329) | copy-start | bytes 9220
  113.7 38.8 %copy-start.34 = (bf16[4,384]{1,0:T(4,128)(2,1)S(1)}, bf16[4,384]{1,0:T(4,128)(2,1)}, u32[]{:S(2)}) copy-start(bf16[4,384]{1,0:T(4,128)(2,1)} %convert_element_type.326) | copy-start | bytes 9220
  113.7 38.8 %copy-start.35 = (bf16[4,384]{1,0:T(4,128)(2,1)S(1)}, bf16[4,384]{1,0:T(4,128)(2,1)}, u32[]{:S(2)}) copy-start(bf16[4,384]{1,0:T(4,128)(2,1)} %convert_element_type.323) | copy-start | bytes 9220
  113.7 38.8 %copy-start.36 = (bf16[4,384]{1,0:T(4,128)(2,1)S(1)}, bf16[4,384]{1,0:T(4,128)(2,1)}, u32[]{:S(2)}) copy-start(bf16[4,384]{1,0:T(4,128)(2,1)} %convert_element_type.320) | copy-start | bytes 9220
  113.7 38.8 %copy-start.37 = (bf16[4,384]{1,0:T(4,128)(2,1)S(1)}, bf16[4,384]{1,0:T(4,128)(2,1)}, u32[]{:S(2)}) copy-start(bf16[4,384]{1,0:T(4,128)(2,1)} %convert_element_type.317) | copy-start | bytes 9220
  113.8 38.8 %copy-start.38 = (bf16[4,384]{1,0:T(4,128)(2,1)S(1)}, bf16[4,384]{1,0:T(4,128)(2,1)}, u32[]{:S(2)}) copy-start(bf16[4,384]{1,0:T(4,128)(2,1)} %convert_element_type.314) | copy-start | bytes 9220
  113.8 38.8 %copy-start.39 = (bf16[4,384]{1,0:T(4,128)(2,1)S(1)}, bf16[4,384]{1,0:T(4,128)(2,1)}, u32[]{:S(2)}) copy-start(bf16[4,384]{1,0:T(4,128)(2,1)} %convert_element_type.311) | copy-start | bytes 9220
  113.9 38.7 %copy-start.40 = (bf16[4,384]{1,0:T(4,128)(2,1)S(1)}, bf16[4,384]{1,0:T(4,128)(2,1)}, u32[]{:S(2)}) copy-start(bf16[4,384]{1,0:T(4,128)(2,1)} %convert_element_type.307) | copy-start | bytes 9220
  114.0 40.3 %copy-start.23 = (f32[384,4]{0,1:T(4,128)}, f32[384,4]{0,1:T(4,128)S(1)}, u32[]{:S(2)}) copy-start(f32[384,4]{0,1:T(4,128)S(1)} %pad_add_fusion.2) | copy-start | bytes 18436
  170.1 189.7 %reduce-scatter.5.cloned.1.call-start = ((), (), s32[]{:S(2)}) async-start(), calls=%async_computation.5 | async-start | bytes 6488064 | tf_op jit(solution)/shard_map/reduce_scatter | solution.py:118
  170.5 7.9 %copy-start.18 = (f32[16,256]{0,1:T(8,128)S(1)}, f32[16,256]{0,1:T(8,128)}, u32[]{:S(2)}) copy-start(f32[16,256]{0,1:T(8,128)} %fusion.49) | copy-start | bytes 49156
  170.5 7.9 %copy-start.19 = (f32[16,256]{0,1:T(8,128)S(1)}, f32[16,256]{0,1:T(8,128)}, u32[]{:S(2)}) copy-start(f32[16,256]{0,1:T(8,128)} %fusion.50) | copy-start | bytes 49156
  170.5 7.9 %copy-start.20 = (f32[16,256]{0,1:T(8,128)S(1)}, f32[16,256]{0,1:T(8,128)}, u32[]{:S(2)}) copy-start(f32[16,256]{0,1:T(8,128)} %fusion.51) | copy-start | bytes 49156
  170.5 7.9 %copy-start.46 = (f32[1,256]{1,0:T(1,128)S(1)}, f32[1,256]{1,0:T(1,128)}, u32[]{:S(2)}) copy-start(f32[1,256]{1,0:T(1,128)} %get-tuple-element.51) | copy-start | bytes 3076
  170.5 7.9 %copy-start.47 = (f32[1,256]{1,0:T(1,128)S(1)}, f32[1,256]{1,0:T(1,128)}, u32[]{:S(2)}) copy-start(f32[1,256]{1,0:T(1,128)} %get-tuple-element.52) | copy-start | bytes 3076
  170.5 7.9 %copy-start.48 = (f32[1,256]{1,0:T(1,128)S(1)}, f32[1,256]{1,0:T(1,128)}, u32[]{:S(2)}) copy-start(f32[1,256]{1,0:T(1,128)} %get-tuple-element.53) | copy-start | bytes 3076
  170.5 7.9 %copy-start.49 = (f32[1,256]{1,0:T(1,128)S(1)}, f32[1,256]{1,0:T(1,128)}, u32[]{:S(2)}) copy-start(f32[1,256]{1,0:T(1,128)} %get-tuple-element.54) | copy-start | bytes 3076
  170.5 7.9 %copy-start.58 = (f32[256]{0:T(256)S(1)}, f32[256]{0:T(256)}, u32[]{:S(2)}) copy-start(f32[256]{0:T(256)} %param.28) | copy-start | bytes 3076
  178.3 13.9 %copy-start.56 = (s32[384]{0:T(512)S(1)}, s32[384]{0:T(512)}, u32[]{:S(2)}) copy-start(s32[384]{0:T(512)} %get-tuple-element.83) | copy-start | bytes 4612
  178.4 13.9 %copy-start.57 = (s32[384]{0:T(512)S(1)}, s32[384]{0:T(512)}, u32[]{:S(2)}) copy-start(s32[384]{0:T(512)} %get-tuple-element.84) | copy-start | bytes 4612
  178.4 13.9 %copy-start.61 = (pred[384]{0:T(512)(128)(4,1)S(1)}, pred[384]{0:T(512)(128)(4,1)}, u32[]{:S(2)}) copy-start(pred[384]{0:T(512)(128)(4,1)} %fusion.64) | copy-start | bytes 1156
  196.6 7.7 %copy-start.54 = (pred[4]{0:T(512)(128)(4,1)S(1)}, pred[4]{0:T(512)(128)(4,1)}, u32[]{:S(2)}) copy-start(pred[4]{0:T(512)(128)(4,1)} %iota_compare_fusion.8) | copy-start | bytes 16
  196.6 75.0 %copy-start.41 = (f32[256]{0:T(256)S(1)}, f32[256]{0:T(256)}, u32[]{:S(2)}) copy-start(f32[256]{0:T(256)} %param.34) | copy-start | bytes 3076
  278.4 81.4 %copy-start.1 = (bf16[8192,64]{0,1:T(8,128)(2,1)S(1)}, bf16[8192,64]{0,1:T(8,128)(2,1)}, u32[]{:S(2)}) copy-start(bf16[8192,64]{0,1:T(8,128)(2,1)} %param.25) | copy-start | bytes 3145732
  (19 other events, 25.5 us)
Sparse Core Ops, SparseCore 0:
  9.5 56.9 all-gather.4
  94.2 41.9 all-gather.6
  170.2 21.0 reduce-scatter.2
  278.5 81.1 reduce-scatter.4

commit v2 on v1

v2 whole, which is shorter than its diff:
```python
import jax
import jax.numpy as jnp
from jax import lax
from jax.experimental import pallas as pl
from jax.experimental.pallas import tpu as pltpu
from jax.sharding import PartitionSpec as P

STEPS = 24
LP = 16
ROWS = STEPS * LP
HALF = ROWS // 2
TROWS = ROWS + 16
THALF = 208
LANES = 256
F32 = jnp.float32
BF16 = jnp.bfloat16
MESH = pl.DeviceIdType.MESH
NT = (((1,), (1,)), ((), ()))


def silu(v):
    return v / (1.0 + jnp.exp(-v))


def rel(j):
    return j + j // 2 - 2 * (j // 3)


def rcopy(src, dst, ssem, rsem, dev):
    return pltpu.make_async_remote_copy(
        src_ref=src,
        dst_ref=dst,
        send_sem=ssem,
        recv_sem=rsem,
        device_id=dev,
        device_id_type=MESH,
    )


def kernel(
    x_ref,
    pack,
    hist,
    hsel,
    par,
    step_t,
    v_hbm,
    mix_hbm,
    out_hbm,
    st_hbm,
    out_ref,
    tok,
    vraw,
    w,
    ms,
    wout,
    st,
    sbf,
    acc,
    accm,
    ss,
    hall,
    mixsend,
    mixrecv,
    bmat,
    cmat,
    cre,
    usend,
    urecv,
    uown,
    sv4,
    m4,
    gated,
    sqs,
    scaled,
    sbuf,
    rbuf,
    hsend,
    hrecv,
    fsend,
    frecv,
    rsum,
    load_sem,
    a_send,
    a_recv,
    as_send,
    as_recv,
    h_send,
    h_recv,
    m_send,
    m_recv,
    c_send,
    c_recv,
    u_send,
    u_recv,
    q_send,
    q_recv,
    r_send,
    r_recv,
    rs_send,
    rs_recv,
):
    d = lax.axis_index("dom")
    me = lax.axis_index("head")
    c = me % 2
    y = (me // 2) % 4
    z = me // 8
    s1 = 8 - 6 * c
    s2 = 2 + 6 * c
    p1 = z * (1 - c) + y * c
    p2 = y * (1 - c) + z * c
    sib = me + 1 - 2 * c

    def head(a, b):
        return {"head": a * s1 + b * s2 + c}

    def slot_own(i, k):
        return ((p1 + rel(i)) % 4) * s1 + ((p2 + rel(k)) % 4) * s2 + c

    def slot_sib(i, k):
        return ((p2 + rel(i)) % 4) * s2 + ((p1 + rel(k)) % 4) * s1 + 1 - c

    next1, prev1 = head((p1 + 1) % 4, p2), head((p1 + 3) % 4, p2)
    next2, prev2 = head(p1, (p2 + 1) % 4), head(p1, (p2 + 3) % 4)
    sibling = {"head": sib}

    def dom(o):
        return {"dom": (d + o) % 4}

    loads = []
    for i in range(8):
        rows = pl.ds(i * 4096, 4096)
        loads.append(
            pltpu.make_async_copy(v_hbm.at[rows], vraw.at[rows], load_sem.at[i])
        )
    loads.append(
        pltpu.make_async_copy(mix_hbm, ms.at[pl.ds(0, 64)], load_sem.at[8])
    )
    loads.append(pltpu.make_async_copy(st_hbm, st, load_sem.at[9]))
    loads.append(pltpu.make_async_copy(out_hbm, wout, load_sem.at[10]))
    for load in loads:
        load.start()

    barrier = pltpu.get_barrier_semaphore()

    @pl.loop(1, 32)
    def _(o):
        pl.semaphore_signal(
            barrier, inc=1, device_id={"head": (me + o) % 32}, device_id_type=MESH
        )

    for o in (1, 2, 3):
        pl.semaphore_signal(barrier, inc=1, device_id=dom(o), device_id_type=MESH)

    tok[me, 0:ROWS] = x_ref[...]
    tok[me, ROWS:TROWS] = jnp.broadcast_to(pack[7:8, :], (16, LANES)).astype(BF16)
    acc[...] = jnp.zeros_like(acc)
    accm[...] = jnp.zeros_like(accm)
    ss[...] = jnp.zeros_like(ss)
    ms[64:80, :] = step_t[...]
    ms[80:128, :] = jnp.zeros((48, 8192), BF16)
    hall[d] = hist[...]
    pl.semaphore_wait(barrier, 34)

    def ring(grp, idx, recv):
        k = (2, 1, 3, 3)[idx] if recv else (0, 0, 2, 1)[idx]
        slot = slot_own(k, 0) if grp == 4 else slot_own(grp, k)
        rows = (pl.ds(0, TROWS), pl.ds(0, TROWS), pl.ds(0, THALF), pl.ds(THALF, TROWS - THALF))[idx]
        to = (next1, prev1) if grp == 4 else (next2, prev2)
        ref = tok.at[slot, rows]
        return rcopy(ref, ref, a_send.at[grp, idx], a_recv.at[grp, idx], to[idx % 2])

    def to_sib(i, k, recv=False):
        slot = slot_sib(i, k) if recv else slot_own(i, k)
        ref = tok.at[slot]
        return rcopy(ref, ref, as_send.at[i * 4 + k], as_recv.at[i * 4 + k], sibling)

    ring(4, 0, False).start()
    ring(4, 1, False).start()
    ring(0, 0, False).start()
    ring(0, 1, False).start()
    to_sib(0, 0).start()

    hcopies = [
        rcopy(hall.at[d], hall.at[d], h_send.at[o - 1], h_recv.at[o - 1], dom(o))
        for o in (1, 2, 3)
    ]
    for copy in hcopies:
        copy.start()

    ri = lax.broadcasted_iota(jnp.int32, (256, 256), 0)
    ci = lax.broadcasted_iota(jnp.int32, (256, 256), 1)
    perm = (ci == 4 * (ri % 64) + ri // 64).astype(F32).astype(BF16)

    def split(b, _):
        v0 = pl.multiple_of(b * 512, 512)
        pair = jnp.concatenate(
            [vraw[pl.ds(v0, 256), :], vraw[pl.ds(v0 + 256, 256), :]], axis=1
        )
        res = jnp.dot(perm, pair, preferred_element_type=F32).astype(BF16)
        k0 = pl.multiple_of(b * 128, 128)
        for n in range(2):
            for j in range(2):
                for r in range(2):
                    m = 64 * (2 * j + r)
                    lane = 256 * r + 128 * j
                    w[pl.ds(k0 + 64 * n, 64), lane : lane + 128] = res[
                        m : m + 64, 128 * n : 128 * n + 128
                    ]
        return 0

    for i in range(4):
        loads[i].wait()
    lax.fori_loop(0, 32, split, 0)

    for idx, k in ((0, 2), (1, 1)):
        ring(4, idx, True).wait_recv()
        ring(4, 2 + idx, False).start()
        ring(k, 0, False).start()
        ring(k, 1, False).start()
        to_sib(k, 0).start()
    for i in range(4, 8):
        loads[i].wait()
    lax.fori_loop(32, 64, split, 0)
    for idx, k in ((0, 2), (1, 1)):
        ring(0, idx, True).wait_recv()
        ring(0, 2 + idx, False).start()
        to_sib(0, k).start()
    ring(4, 2, True).wait_recv()
    ring(4, 3, True).wait_recv()
    ring(3, 0, False).start()
    ring(3, 1, False).start()
    to_sib(3, 0).start()

    loads[8].wait()

    def project(slot):
        xf = tok[slot, 0:ROWS].astype(F32)
        grow = tok[slot, ROWS:TROWS].astype(F32)[0:1]
        sq = xf * xf
        ss[...] += sq[:, 0:128] + sq[:, 128:256]
        xg = (xf * grow).astype(BF16)
        k0 = pl.multiple_of(slot * 256, 256)
        acc[...] += jnp.dot(xg, w[pl.ds(k0, 256), :], preferred_element_type=F32)
        accm[...] += lax.dot_general(
            xg, ms[:, pl.ds(k0, 256)], NT, preferred_element_type=F32
        )

    def batch(count, which):
        def one(b, _):
            i, k = which(b // 2)
            side = b % 2

            @pl.when(side == 1)
            def _():
                to_sib(i, k, True).wait_recv()

            project(slot_own(i, k) * (1 - side) + slot_sib(i, k) * side)
            return 0

        lax.fori_loop(0, 2 * count, one, 0)

    loads[9].wait()

    def cast(q, _):
        sbf[:, pl.ds(pl.multiple_of(q * 256, 256), 256)] = st[q].astype(BF16)
        return 0

    lax.fori_loop(0, LP, cast, 0)
    batch(4, lambda b: (b, 0))
    for i in (1, 2):
        for idx, k in ((0, 2), (1, 1)):
            ring(i, idx, True).wait_recv()
            ring(i, 2 + idx, False).start()
            to_sib(i, k).start()
    ring(0, 2, True).wait_recv()
    ring(0, 3, True).wait_recv()
    to_sib(0, 3).start()
    batch(3, lambda b: (0, b + 1))
    for idx, k in ((0, 2), (1, 1)):
        ring(3, idx, True).wait_recv()
        ring(3, 2 + idx, False).start()
        to_sib(3, k).start()
    for i in (1, 2):
        ring(i, 2, True).wait_recv()
        ring(i, 3, True).wait_recv()
        to_sib(i, 3).start()
    batch(6, lambda b: (1 + b // 3, 1 + b % 3))
    batch(2, lambda b: (3, 1 + b))
    ring(3, 2, True).wait_recv()
    ring(3, 3, True).wait_recv()
    to_sib(3, 3).start()
    batch(1, lambda b: (3 + b, 3))

    inv = lax.rsqrt(jnp.sum(ss[...], axis=1, keepdims=True) / 8192.0 + 1e-5)

    for copy in hcopies:
        copy.wait()
    hprev = jnp.dot(
        hsel[...], hall[...].reshape(192, 384), preferred_element_type=F32
    )
    mtile = accm[...] * inv

    def conv(window, k0, bias, width):
        total = pack[bias : bias + 1, 0:width]
        for k in range(4):
            total = total + pack[k0 + k : k0 + k + 1, 0:width] * window[
                k * LP : k * LP + ROWS
            ]
        return silu(total)

    mact = conv(jnp.concatenate([hprev[:, 256:384], mtile], 0), 8, 12, 128)
    low = lax.broadcasted_iota(jnp.int32, (HALF, 128), 1) < 64
    mixsend[...] = jnp.where(
        low, mact[0:HALF], pltpu.roll(mact[HALF:ROWS], 64, 1)
    ).astype(BF16)
    first = ((me % 16) // 4) * 8
    place = (me // 16) * 4 + me % 4

    def mix_copy(n):
        return rcopy(
            mixsend, mixrecv.at[place], m_send.at[n], m_recv.at[place], {"head": first + n}
        )

    @pl.loop(0, 8)
    def _(n):
        @pl.when(first + n != me)
        def _():
            mix_copy(n).start()

        @pl.when(first + n == me)
        def _():
            pltpu.make_async_copy(mixsend, mixrecv.at[place], m_recv.at[place]).start()

    value = acc[:, 256:512] * inv
    vact = conv(jnp.concatenate([hprev[:, 0:256], value], 0), 0, 4, 256)
    gact = silu(acc[:, 0:256] * inv)
    step = mtile + pack[13:14, 0:128]
    step = jnp.maximum(step, 0.0) + jnp.log1p(jnp.exp(-jnp.abs(step)))
    run = -step * pack[14:15, 0:128]
    for sh in (1, 2, 4, 8, 16):
        z0 = jnp.zeros((sh * LP, 128), F32)
        run = run + jnp.concatenate([z0, run[: ROWS - sh * LP]], 0)
    run_t = run.T
    lane = lax.broadcasted_iota(jnp.int32, (ROWS, LANES), 1)

    def spread(t):
        out = jnp.broadcast_to(t[:, 67:68], (ROWS, LANES))
        for h in (2, 1, 0):
            out = jnp.where(lane < 64 * h + 64, t[:, 64 + h : 65 + h], out)
        return out

    sv = vact * spread(step)
    for h in range(4):
        inside = (lane >= 64 * h) & (lane < 64 * h + 64)
        sv4[h * ROWS : (h + 1) * ROWS, :] = jnp.where(inside, sv, 0.0).astype(BF16)

    @pl.loop(0, 8)
    def _(n):
        rcopy(mixsend, mixrecv.at[n], m_send.at[n], m_recv.at[n], sibling).wait_recv()

    def assemble(first_slot, dst):
        for t in range(2):
            a = mixrecv[first_slot + 2 * t].astype(F32)
            b = mixrecv[first_slot + 2 * t + 1].astype(F32)
            dst[0:HALF, 128 * t : 128 * t + 128] = jnp.where(
                low, a, pltpu.roll(b, 64, 1)
            ).astype(BF16)
            dst[HALF:ROWS, 128 * t : 128 * t + 128] = jnp.where(
                low, pltpu.roll(a, 64, 1), b
            ).astype(BF16)

    assemble(4, cmat)
    ccopies = [
        rcopy(cmat, cre.at[o - 1], c_send.at[o - 1], c_recv.at[o - 1], dom(o))
        for o in (1, 2, 3)
    ]
    for copy in ccopies:
        copy.start()
    assemble(0, bmat)

    gram = lax.dot_general(cmat[...], bmat[...], NT, preferred_element_type=F32)
    gi = lax.broadcasted_iota(jnp.int32, (ROWS, ROWS), 0)
    gj = lax.broadcasted_iota(jnp.int32, (ROWS, ROWS), 1)
    keep = ((gi % LP) == (gj % LP)) & (gj <= gi)
    for h in range(4):
        diff = jnp.where(keep, run[:, 64 + h : 65 + h] - run_t[64 + h : 65 + h, :], -1e30)
        m4[:, h * ROWS : (h + 1) * ROWS] = (gram * jnp.exp(diff)).astype(BF16)
    inner = jnp.dot(m4[...], sv4[...], preferred_element_type=F32)

    def reads(cref, e):
        def part(n, u):
            cval = cref[...].reshape(STEPS, LP, LANES)
            mine = par[pl.ds(pl.multiple_of(e * LP, LP), LP), :]
            lhs = []
            for t in range(4):
                q = (d * LP + n * 4 + t).astype(F32)
                mask = jnp.where(mine == q, 1.0, 0.0).astype(BF16)
                lhs.append((cval * mask[None]).reshape(ROWS, LANES))
            return u + lax.dot_general(
                jnp.concatenate(lhs, 1),
                sbf[:, pl.ds(pl.multiple_of(n * 1024, 1024), 1024)],
                NT,
                preferred_element_type=F32,
            )

        return lax.fori_loop(0, 4, part, jnp.zeros((ROWS, LANES), F32))

    ucopies = []
    for o in (1, 3, 2):
        ccopies[o - 1].wait_recv()
        usend[o - 1] = reads(cre.at[o - 1], (d + 4 - o) % 4).astype(BF16)
        ucopies.append(
            rcopy(usend.at[o - 1], urecv.at[o - 1], u_send.at[o - 1], u_recv.at[o - 1], dom(4 - o))
        )
        ucopies[-1].start()
    start_read = reads(cmat, d)
    for copy in ucopies:
        copy.wait_recv()
    for o in range(3):
        start_read = start_read + urecv[o].astype(F32)
    total = inner + jnp.exp(spread(run)) * start_read + pack[5:6, :] * vact
    total = total * gact
    sq = lax.dot_general(
        jnp.ones((8, LANES), F32),
        total * total,
        NT,
        preferred_element_type=F32,
        precision=lax.Precision.HIGHEST,
    )
    place8 = me % 8
    sqs[place8] = sq

    def sq_copy(o):
        at = (place8 + o) % 8
        return rcopy(
            sqs.at[place8], sqs.at[place8], q_send.at[o - 1], q_recv.at[o - 1], {"head": z * 8 + at}
        )

    for o in range(1, 8):
        sq_copy(o).start()
    for o in range(1, 8):
        at = (place8 + 8 - o) % 8
        rcopy(sqs.at[at], sqs.at[at], q_send.at[o - 1], q_recv.at[o - 1], sibling).wait_recv()
    tsq = sqs[0]
    for o in range(1, 8):
        tsq = tsq + sqs[o]
    inv2 = lax.rsqrt(tsq.T[:, 0:1] / 2048.0 + 1e-5)
    scaled[...] = (total * inv2 * pack[6:7, :]).astype(BF16)

    loads[10].wait()

    def terms(slot):
        return jnp.dot(
            scaled[...],
            wout[:, pl.ds(pl.multiple_of(slot * 256, 256), 256)],
            preferred_element_type=F32,
        )

    def sib_terms(n):
        return rcopy(sbuf.at[n], rbuf.at[n], rs_send.at[n], rs_recv.at[n], sibling)

    @pl.loop(0, 16)
    def _(t):
        n = (3 - t % 4) * 4 + 3 - t // 4
        sbuf[n] = terms(slot_sib(n // 4, n % 4)).astype(BF16)
        sib_terms(n).start()

    def mine(i, k):
        sib_terms(i * 4 + k).wait_recv()
        return terms(slot_own(i, k)) + rbuf[i * 4 + k].astype(F32)

    def half_copy(i, top, to):
        rows = pl.ds(0 if top else HALF, HALF)
        n = 0 if top else 1
        return rcopy(hsend.at[i, rows], hrecv.at[i, rows], r_send.at[i, n], r_recv.at[i, n], to)

    def full_copy(i, n, to):
        return rcopy(
            fsend.at[2 * i + n], frecv.at[2 * i + n], r_send.at[i, 2 + n], r_recv.at[i, 2 + n], to
        )

    @pl.loop(0, 4)
    def _(t):
        i = 3 - t
        hsend[i] = mine(i, 3).astype(BF16)
        half_copy(i, True, next2).start()
        half_copy(i, False, prev2).start()

    @pl.loop(0, 4)
    def _(t):
        i = 3 - t
        a = mine(i, 1)
        half_copy(i, True, next2).wait_recv()
        fsend[2 * i, 0:HALF] = (a[0:HALF] + hrecv[i, 0:HALF].astype(F32)).astype(BF16)
        fsend[2 * i, HALF:ROWS] = a[HALF:ROWS].astype(BF16)
        full_copy(i, 0, next2).start()
        b = mine(i, 2)
        half_copy(i, False, prev2).wait_recv()
        fsend[2 * i + 1, 0:HALF] = b[0:HALF].astype(BF16)
        fsend[2 * i + 1, HALF:ROWS] = (
            b[HALF:ROWS] + hrecv[i, HALF:ROWS].astype(F32)
        ).astype(BF16)
        full_copy(i, 1, prev2).start()

    @pl.loop(0, 4)
    def _(t):
        i = 3 - t
        a = mine(i, 0)
        full_copy(i, 0, next2).wait_recv()
        full_copy(i, 1, prev2).wait_recv()
        a = a + frecv[2 * i].astype(F32) + frecv[2 * i + 1].astype(F32)
        rsum[i] = a

        @pl.when(i == 3)
        def _():
            hsend[4] = a.astype(BF16)
            half_copy(4, True, next1).start()
            half_copy(4, False, prev1).start()

    half_copy(4, True, next1).wait_recv()
    fsend[8, 0:HALF] = (rsum[1, 0:HALF] + hrecv[4, 0:HALF].astype(F32)).astype(BF16)
    fsend[8, HALF:ROWS] = rsum[1, HALF:ROWS].astype(BF16)
    full_copy(4, 0, next1).start()
    half_copy(4, False, prev1).wait_recv()
    fsend[9, 0:HALF] = rsum[2, 0:HALF].astype(BF16)
    fsend[9, HALF:ROWS] = (
        rsum[2, HALF:ROWS] + hrecv[4, HALF:ROWS].astype(F32)
    ).astype(BF16)
    full_copy(4, 1, prev1).start()
    full_copy(4, 0, next1).wait_recv()
    full_copy(4, 1, prev1).wait_recv()
    out_ref[...] = (rsum[0] + frecv[8].astype(F32) + frecv[9].astype(F32)).astype(BF16)

    for grp in range(5):
        for idx in range(4):
            ring(grp, idx, False).wait_send()

    @pl.loop(0, 16)
    def _(n):
        to_sib(n // 4, n % 4).wait_send()
        sib_terms(n).wait_send()

    @pl.loop(0, 8)
    def _(n):
        @pl.when(first + n != me)
        def _():
            mix_copy(n).wait_send()

    for copy in ccopies + ucopies:
        copy.wait_send()
    for o in range(1, 8):
        sq_copy(o).wait_send()
    for i in range(5):
        nxt, prv = (next1, prev1) if i == 4 else (next2, prev2)
        half_copy(i, True, nxt).wait_send()
        half_copy(i, False, prv).wait_send()
        full_copy(i, 0, nxt).wait_send()
        full_copy(i, 1, prv).wait_send()


def body(
    tokens,
    parents,
    state,
    vhist,
    mhist,
    gain,
    gvw,
    mw,
    sw,
    vk,
    vo,
    mk,
    mo,
    so,
    dlog,
    skip,
    ogain,
    ow,
):
    d = lax.axis_index("dom")

    def wide(a, at=0):
        a = a.reshape(-1, a.shape[-1])
        return jnp.pad(a, ((0, 0), (at, 256 - at - a.shape[-1])))

    pack = jnp.concatenate(
        [
            vk,
            wide(vo),
            jnp.repeat(skip, 64)[None],
            wide(ogain),
            wide(gain),
            wide(mk),
            wide(mo),
            wide(so, 64),
            wide(jnp.exp(dlog), 64),
            jnp.zeros((1, 256), F32),
        ],
        0,
    )
    hist = jnp.concatenate(
        [
            jnp.moveaxis(vhist, 1, 0),
            jnp.pad(jnp.moveaxis(mhist, 1, 0), ((0, 0), (0, 0), (0, 64))),
        ],
        2,
    )
    hist = hist.astype(BF16).reshape(48, 384)
    own = lax.dynamic_slice_in_dim(parents, d * LP, LP)
    a = jnp.arange(48)[:, None]
    b = jnp.arange(192)[None, :]
    hsel = (
        (a // LP == (b // LP) % 3)
        & (jnp.tile(own, 3)[:, None] == (b // 48) * LP + b % LP)
    ).astype(BF16)
    par = jnp.broadcast_to(parents.astype(F32)[:, None], (64, 256))
    step_t = jnp.pad(sw.T, ((0, 12), (0, 0)))
    v = gvw.reshape(8192, 2, 2, 128).transpose(0, 2, 1, 3).reshape(32768, 128)

    vmem = pl.BlockSpec(memory_space=pltpu.VMEM)
    hbm = pl.BlockSpec(memory_space=pl.ANY)
    dma = pltpu.SemaphoreType.DMA
    big = (ROWS, LANES)
    out = pl.pallas_call(
        kernel,
        out_shape=jax.ShapeDtypeStruct(big, BF16),
        in_specs=[vmem] * 6 + [hbm] * 4,
        out_specs=vmem,
        scratch_shapes=[
            pltpu.VMEM((32, TROWS, LANES), BF16),
            pltpu.VMEM((32768, 128), BF16),
            pltpu.VMEM((8192, 512), BF16),
            pltpu.VMEM((128, 8192), BF16),
            pltpu.VMEM((256, 8192), BF16),
            pltpu.VMEM((LP, 256, 256), F32),
            pltpu.VMEM((256, LP * 256), BF16),
            pltpu.VMEM((ROWS, 512), F32),
            pltpu.VMEM((ROWS, 128), F32),
            pltpu.VMEM((ROWS, 128), F32),
            pltpu.VMEM((4, 48, 384), BF16),
            pltpu.VMEM((HALF, 128), BF16),
            pltpu.VMEM((8, HALF, 128), BF16),
            pltpu.VMEM(big, BF16),
            pltpu.VMEM(big, BF16),
            pltpu.VMEM((3, *big), BF16),
            pltpu.VMEM((3, *big), BF16),
            pltpu.VMEM((3, *big), BF16),
            pltpu.VMEM((8, 128), F32),
            pltpu.VMEM((4 * ROWS, LANES), BF16),
            pltpu.VMEM((ROWS, 4 * ROWS), BF16),
            pltpu.VMEM((8, 128), F32),
            pltpu.VMEM((8, 8, ROWS), F32),
            pltpu.VMEM(big, BF16),
            pltpu.VMEM((16, *big), BF16),
            pltpu.VMEM((16, *big), BF16),
            pltpu.VMEM((5, *big), BF16),
            pltpu.VMEM((5, *big), BF16),
            pltpu.VMEM((10, *big), BF16),
            pltpu.VMEM((10, *big), BF16),
            pltpu.VMEM((4, *big), F32),
            dma((11,)),
            dma((5, 4)),
            dma((5, 4)),
            dma((16,)),
            dma((16,)),
            dma((3,)),
            dma((3,)),
            dma((8,)),
            dma((8,)),
            dma((3,)),
            dma((3,)),
            dma((3,)),
            dma((3,)),
            dma((7,)),
            dma((7,)),
            dma((5, 4)),
            dma((5, 4)),
            dma((16,)),
            dma((16,)),
        ],
        compiler_params=pltpu.CompilerParams(
            collective_id=0,
            has_side_effects=True,
            vmem_limit_bytes=63 * 1024 * 1024,
        ),
    )(
        tokens.reshape(ROWS, LANES),
        pack,
        hist,
        hsel,
        par,
        step_t,
        v,
        mw.T,
        ow,
        state.reshape(LP, 256, 256),
    )
    return out.reshape(STEPS, LP, LANES)


def solution(mesh):
    return jax.shard_map(
        body,
        mesh=mesh,
        in_specs=(
            P(None, "dom", "head"),
            P(),
            P("dom", "head", None, None),
            P("dom", None, "head"),
            P("dom", None, "head"),
            P("head"),
            P(None, None, "head"),
            P(None, "head"),
            P(None, "head"),
            P(None, "head"),
            P("head"),
            P(None, "head"),
            P("head"),
            P("head"),
            P("head"),
            P("head"),
            P("head"),
            P("head", None),
        ),
        out_specs=P(None, "dom", "head"),
        check_vma=False,
    )
```

time: 367 us -> 118 us (0.32)
  blocking collectives: 132 us -> 0 us
  waiting for transfers between devices: 115 us -> 0 us
  Pallas kernels: 0 us -> 104 us
  matrix products: 43.2 us -> 0 us
  local copies, waits for them, and re-layouts: 43.2 us -> 10.3 us
  other arithmetic: 18 us -> 3.52 us
  between operations: 14.3 us -> 0.02 us
    pallas_call x0 -> x1, Pallas kernels: none -> 104 us  [body(): pl.pallas_call(kernel, out_shape=jax.ShapeDtypeStruct(big, BF16), in_spec...]
    reduce_scatter x2 -> x0, waiting for transfers between devices: 92.2 us -> none  [the longest x1 81.4 us: body(): out = lax.psum_scatter(terms, 'head', scatter_dimension=1, tiled=True)]
    psum x1 -> x0, blocking collectives: 67.2 us -> none  [body(): lax.psum(jnp.where(jnp.arange(GROUPS)[:, None] == g, sq[None, :], 0.0), '...]
    all_gather x4 -> x0, blocking collectives: 64.8 us -> none  [the longest x1 25.7 us: body(): lax.all_gather(gain.astype(BF16), 'head', axis=0, tiled=True).astype(F32)]
    dot_general x32 -> x0, matrix products: 43.2 us -> none  [the longest x1 7.78 us: body(): value = jnp.dot(normed, gvw[:, 1, :], preferred_element_type=F32)]
    all_gather x2 -> x0, waiting for transfers between devices: 22.3 us -> none  [the longest x1 22.3 us: body(): mixall = lax.all_gather(mact.astype(BF16), 'head', axis=1, tiled=True)]
    slice x8 -> x0, local copies, waits for them, and re-layouts: 20.1 us -> none  [the longest x1 17.6 us: body(): gate = jnp.dot(normed, gvw[:, 0, :], preferred_element_type=F32)]
    convert_element_type x32 -> x0, local copies, waits for them, and re-layouts: 9.97 us -> none  [body(): mask = (row_parent == d * LP + q).astype(BF16)[:, None]]
  transfers between devices with their start and end apart: 4 -> 0, of which waited for: 3 -> 0; matrix products, arithmetic and copies ran while one was open for 15% -> 0% of each run, Pallas kernels for 0% -> 0%
where the time goes in v2:
time: 118 us
  Pallas kernels  104 us (88%)
  local copies, waits for them, and re-layouts  10.3 us (9%)
  other arithmetic  3.52 us (3%)
    pallas_call x1, Pallas kernels, body(): pl.pallas_call(kernel, out_shape=jax.ShapeDtypeStruct(big, BF16), in_spec...  104 us

profile of v2, /device:TPU:0, one launch (start us, length us, event | category | flops | bytes accessed | tf_op | source)
XLA Modules:
  0.0 117.8 jit_solution(7590700882037733231)
XLA Ops:
  0.0 0.7 dynamic_slice.3
  0.7 0.7 exponential_bitcast_fusion
  1.4 0.1 pad.27
  1.5 0.7 convert_element_type.20
  2.1 0.7 pad.25
  2.8 0.7 pad.26
  3.5 0.1 eq.34
  3.6 0.7 broadcast_in_dim.6
  4.3 0.1 broadcast_in_dim_reshape.3
  4.4 0.7 pad.24
  5.1 1.9 %concatenate.12.pack = f32[16,256]{1,0:T(8,128)} concatenate(f32[4,256]{1,0:T(4,128)} %param.27, f32[1,256]{1,0:T(1,128)} %bitcast.31, f32[1,256]{1,0:T(1,128)S(1)} %broadcast_in_dim_reshape.3, f32[1,256]{1,0:T(1,128)} %bitcast.32, f32[1,256]{1,0:T(1,128)} %bitcast.33, f32[4,256]{1,0:T(4,128)S(1)} %pad.24, f32[1,256]{1,0:T(1,128)S(1)} %pad.25, f32[1,256]{1,0:T(1,128)S(1)} %pad.26, ...), dimensions={0} | concatenate | bytes 32768 | tf_op jit(solution)/shard_map/concatenate | solution.py:588
  7.1 0.7 convert_bitcast_fusion
  7.8 0.7 and_convert_fusion.hsel
  8.5 0.8 convert.12
  9.3 0.6 pad_maximum_fusion.hist
  9.9 0.7 broadcast_in_dim.16.par
  10.6 1.6 %pad.29.step_t = bf16[16,8192]{1,0:T(8,128)(2,1)} pad(bf16[4,8192]{1,0:T(4,128)(2,1)} %bitcast.29, bf16[]{:T(256)} %constant.60.clone.1), padding=0_12x0_0 | pad | bytes 327682 | tf_op jit(solution)/shard_map/jit(_pad)/pad | solution.py:619
  12.2 104.0 %shard_map.172 = bf16[384,256]{1,0:T(8,128)(2,1)} custom-call(bf16[384,256]{1,0:T(8,128)(2,1)} %bitcast.27, f32[16,256]{1,0:T(8,128)} %concatenate.12.pack, bf16[48,384]{1,0:T(8,128)(2,1)} %pad_maximum_fusion.hist, bf16[48,192]{1,0:T(8,128)(2,1)} %and_convert_fusion.hsel, f32[64,256]{1,0:T(8,128)} %broadcast_in_dim.16.par, bf16[16,8192]{1,0:T(8,128)(2,1)} %pad.29.step_t, ...), custom_call_target="tpu_custom_call" | custom-call | tf_op jit(solution)/shard_map/pallas_call | solution.py:626
  116.2 1.6 %copy.21 = bf16[24,16,256]{2,1,0:T(8,128)(2,1)} copy(bf16[24,16,256]{2,1,0:T(8,128)(2,1)} %bitcast.26) | data formatting | bytes 393216
  (5 shorter events, 0.0 us)

commit v3 on v2

--- a/solution.py
+++ b/solution.py
@@ -38,17 +38,39 @@
 
 
 def kernel(
-    x_ref,
-    pack,
-    hist,
-    hsel,
-    par,
-    step_t,
+    x_hbm,
+    parents_hbm,
+    vh_hbm,
+    mh_hbm,
+    gain_hbm,
+    vk_hbm,
+    vo_hbm,
+    mk_hbm,
+    mo_hbm,
+    so_hbm,
+    dlog_hbm,
+    skip_hbm,
+    ogain_hbm,
+    step_hbm,
     v_hbm,
     mix_hbm,
     out_hbm,
     st_hbm,
     out_ref,
+    parents,
+    vh,
+    mh,
+    gain,
+    vk,
+    vo,
+    mk,
+    mo,
+    so,
+    dlog,
+    skip,
+    ogain,
+    step_w,
+    par,
     tok,
     vraw,
     w,
@@ -63,16 +85,16 @@
     mixsend,
     mixrecv,
     bmat,
-    cmat,
-    cre,
+    call,
+    ufar,
+    ufarr,
     usend,
     urecv,
-    uown,
     sv4,
     m4,
-    gated,
     sqs,
     scaled,
+    inv2s,
     sbuf,
     rbuf,
     hsend,
@@ -81,6 +103,7 @@
     frecv,
     rsum,
     load_sem,
+    small_sem,
     a_send,
     a_recv,
     as_send,
@@ -89,8 +112,11 @@
     h_recv,
     m_send,
     m_recv,
+    mf_send,
     c_send,
     c_recv,
+    cs_send,
+    cs_recv,
     u_send,
     u_recv,
     q_send,
@@ -127,6 +153,34 @@
     def dom(o):
         return {"dom": (d + o) % 4}
 
+    small = [
+        pltpu.make_async_copy(src, dst, small_sem.at[n])
+        for n, (src, dst) in enumerate(
+            (
+                (x_hbm, tok.at[me, pl.ds(0, ROWS)]),
+                (gain_hbm, gain),
+                (parents_hbm, parents),
+                (vh_hbm, vh),
+                (mh_hbm, mh),
+                (vk_hbm, vk),
+                (vo_hbm, vo),
+                (mk_hbm, mk),
+                (mo_hbm, mo),
+                (so_hbm, so),
+                (dlog_hbm, dlog),
+                (skip_hbm, skip),
+                (ogain_hbm, ogain),
+                (step_hbm, step_w),
+            )
+        )
+    ]
+    for load in small:
+        load.start()
+
+    barrier = pltpu.get_barrier_semaphore()
+    for dev in (next1, prev1, next2, prev2, sibling, dom(1), dom(2), dom(3)):
+        pl.semaphore_signal(barrier, inc=1, device_id=dev, device_id_type=MESH)
+
     loads = []
     for i in range(8):
         rows = pl.ds(i * 4096, 4096)
@@ -140,27 +194,16 @@
     loads.append(pltpu.make_async_copy(out_hbm, wout, load_sem.at[10]))
     for load in loads:
         load.start()
-
-    barrier = pltpu.get_barrier_semaphore()
-
-    @pl.loop(1, 32)
-    def _(o):
-        pl.semaphore_signal(
-            barrier, inc=1, device_id={"head": (me + o) % 32}, device_id_type=MESH
-        )
-
-    for o in (1, 2, 3):
-        pl.semaphore_signal(barrier, inc=1, device_id=dom(o), device_id_type=MESH)
-
-    tok[me, 0:ROWS] = x_ref[...]
-    tok[me, ROWS:TROWS] = jnp.broadcast_to(pack[7:8, :], (16, LANES)).astype(BF16)
-    acc[...] = jnp.zeros_like(acc)
-    accm[...] = jnp.zeros_like(accm)
-    ss[...] = jnp.zeros_like(ss)
-    ms[64:80, :] = step_t[...]
-    ms[80:128, :] = jnp.zeros((48, 8192), BF16)
-    hall[d] = hist[...]
-    pl.semaphore_wait(barrier, 34)
+    for load in small:
+        load.wait()
+    tok[me, ROWS:TROWS] = jnp.broadcast_to(gain[...], (16, LANES)).astype(BF16)
+    for n in range(3):
+        rows = pl.ds(n * LP, LP)
+        hall[d, rows, 0:256] = vh[rows, :].astype(BF16)
+        hall[d, rows, 256:384] = jnp.concatenate(
+            [mh[rows, :], jnp.zeros((LP, 64), F32)], 1
+        ).astype(BF16)
+    pl.semaphore_wait(barrier, 8)
 
     def ring(grp, idx, recv):
         k = (2, 1, 3, 3)[idx] if recv else (0, 0, 2, 1)[idx]
@@ -187,6 +230,20 @@
     ]
     for copy in hcopies:
         copy.start()
+
+    acc[...] = jnp.zeros_like(acc)
+    accm[...] = jnp.zeros_like(accm)
+    ss[...] = jnp.zeros_like(ss)
+    ms[64:80, :] = jnp.concatenate(
+        [step_w[...].astype(F32), jnp.zeros((12, 8192), F32)], 0
+    ).astype(BF16)
+    ms[80:128, :] = jnp.zeros((48, 8192), BF16)
+    pi = lax.broadcasted_iota(jnp.int32, (64, 64), 0)
+    pj = lax.broadcasted_iota(jnp.int32, (64, 64), 1)
+    par[...] = jnp.broadcast_to(
+        jnp.sum(jnp.where(pi == pj, parents[...].astype(F32), 0.0), 1, keepdims=True),
+        (64, LANES),
+    )
 
     ri = lax.broadcasted_iota(jnp.int32, (256, 256), 0)
     ci = lax.broadcasted_iota(jnp.int32, (256, 256), 1)
@@ -234,130 +291,155 @@
 
     loads[8].wait()
 
-    def project(slot):
-        xf = tok[slot, 0:ROWS].astype(F32)
-        grow = tok[slot, ROWS:TROWS].astype(F32)[0:1]
-        sq = xf * xf
-        ss[...] += sq[:, 0:128] + sq[:, 128:256]
-        xg = (xf * grow).astype(BF16)
-        k0 = pl.multiple_of(slot * 256, 256)
-        acc[...] += jnp.dot(xg, w[pl.ds(k0, 256), :], preferred_element_type=F32)
+    def project(i, k):
+        to_sib(i, k, True).wait_recv()
+        lhs, wide_rhs, narrow_rhs = [], [], []
+        part = ss[...]
+        for slot in (slot_own(i, k), slot_sib(i, k)):
+            xf = tok[slot, 0:ROWS].astype(F32)
+            grow = tok[slot, ROWS:TROWS].astype(F32)[0:1]
+            sq = xf * xf
+            part = part + sq[:, 0:128] + sq[:, 128:256]
+            lhs.append((xf * grow).astype(BF16))
+            k0 = pl.multiple_of(slot * 256, 256)
+            wide_rhs.append(w[pl.ds(k0, 256), :])
+            narrow_rhs.append(ms[:, pl.ds(k0, 256)])
+        ss[...] = part
+        xg = jnp.concatenate(lhs, 1)
+        acc[...] += jnp.dot(
+            xg, jnp.concatenate(wide_rhs, 0), preferred_element_type=F32
+        )
         accm[...] += lax.dot_general(
-            xg, ms[:, pl.ds(k0, 256)], NT, preferred_element_type=F32
+            xg, jnp.concatenate(narrow_rhs, 1), NT, preferred_element_type=F32
         )
 
     def batch(count, which):
         def one(b, _):
-            i, k = which(b // 2)
-            side = b % 2
-
-            @pl.when(side == 1)
-            def _():
-                to_sib(i, k, True).wait_recv()
-
-            project(slot_own(i, k) * (1 - side) + slot_sib(i, k) * side)
+            project(*which(b))
             return 0
 
-        lax.fori_loop(0, 2 * count, one, 0)
-
-    loads[9].wait()
+        lax.fori_loop(0, count, one, 0)
 
     def cast(q, _):
         sbf[:, pl.ds(pl.multiple_of(q * 256, 256), 256)] = st[q].astype(BF16)
         return 0
 
-    lax.fori_loop(0, LP, cast, 0)
-    batch(4, lambda b: (b, 0))
-    for i in (1, 2):
+    def pass_on(i):
         for idx, k in ((0, 2), (1, 1)):
             ring(i, idx, True).wait_recv()
             ring(i, 2 + idx, False).start()
             to_sib(i, k).start()
-    ring(0, 2, True).wait_recv()
-    ring(0, 3, True).wait_recv()
-    to_sib(0, 3).start()
-    batch(3, lambda b: (0, b + 1))
-    for idx, k in ((0, 2), (1, 1)):
-        ring(3, idx, True).wait_recv()
-        ring(3, 2 + idx, False).start()
-        to_sib(3, k).start()
-    for i in (1, 2):
+
+    def far(i):
         ring(i, 2, True).wait_recv()
         ring(i, 3, True).wait_recv()
         to_sib(i, 3).start()
-    batch(6, lambda b: (1 + b // 3, 1 + b % 3))
-    batch(2, lambda b: (3, 1 + b))
-    ring(3, 2, True).wait_recv()
-    ring(3, 3, True).wait_recv()
-    to_sib(3, 3).start()
+
+    batch(1, lambda b: (b, 0))
+    pass_on(1)
+    batch(1, lambda b: (b + 1, 0))
+    pass_on(2)
+    loads[9].wait()
+    lax.fori_loop(0, LP, cast, 0)
+    far(0)
+    batch(2, lambda b: (2 + b, 0))
+    pass_on(3)
+    batch(3, lambda b: (0, b + 1))
+    far(1)
+    batch(2, lambda b: (1, b + 1))
+    far(2)
+    batch(3, lambda b: (1 + (b + 2) // 3, 3 * (1 - (b + 2) // 3) + b))
+    batch(3, lambda b: (2 + (b + 1) // 2, 3 * (1 - (b + 1) // 2) + b))
+    far(3)
     batch(1, lambda b: (3 + b, 3))
 
     inv = lax.rsqrt(jnp.sum(ss[...], axis=1, keepdims=True) / 8192.0 + 1e-5)
 
     for copy in hcopies:
         copy.wait()
-    hprev = jnp.dot(
-        hsel[...], hall[...].reshape(192, 384), preferred_element_type=F32
+    hi = lax.broadcasted_iota(jnp.int32, (LP, 192), 1)
+    same = par[pl.ds(pl.multiple_of(d * LP, LP), LP), 0:192] == (
+        (hi // 48) * LP + hi % LP
+    ).astype(F32)
+    hot = jnp.concatenate(
+        [
+            jnp.where(same & ((hi // LP) % 3 == n), 1.0, 0.0).astype(BF16)
+            for n in range(3)
+        ],
+        0,
     )
+    hprev = jnp.dot(hot, hall[...].reshape(192, 384), preferred_element_type=F32)
     mtile = accm[...] * inv
 
-    def conv(window, k0, bias, width):
-        total = pack[bias : bias + 1, 0:width]
+    def conv(window, taps, bias):
+        total = bias
         for k in range(4):
-            total = total + pack[k0 + k : k0 + k + 1, 0:width] * window[
-                k * LP : k * LP + ROWS
-            ]
+            total = total + taps[k : k + 1] * window[k * LP : k * LP + ROWS]
         return silu(total)
 
-    mact = conv(jnp.concatenate([hprev[:, 256:384], mtile], 0), 8, 12, 128)
+    wide4 = jnp.zeros((4, 64), F32)
+    mact = conv(
+        jnp.concatenate([hprev[:, 256:384], mtile], 0),
+        jnp.concatenate([mk[...], wide4], 1),
+        jnp.concatenate([mo[...], wide4[0:1]], 1),
+    )
     low = lax.broadcasted_iota(jnp.int32, (HALF, 128), 1) < 64
     mixsend[...] = jnp.where(
         low, mact[0:HALF], pltpu.roll(mact[HALF:ROWS], 64, 1)
     ).astype(BF16)
-    first = ((me % 16) // 4) * 8
+    first = ((me % 16) // 4) * 8 + c
     place = (me // 16) * 4 + me % 4
 
     def mix_copy(n):
         return rcopy(
-            mixsend, mixrecv.at[place], m_send.at[n], m_recv.at[place], {"head": first + n}
-        )
-
-    @pl.loop(0, 8)
+            mixsend, mixrecv.at[place], m_send.at[n], m_recv.at[place], {"head": first + 2 * n}
+        )
+
+    @pl.loop(0, 4)
     def _(n):
-        @pl.when(first + n != me)
+        @pl.when(first + 2 * n != me)
         def _():
             mix_copy(n).start()
 
-        @pl.when(first + n == me)
+        @pl.when(first + 2 * n == me)
         def _():
             pltpu.make_async_copy(mixsend, mixrecv.at[place], m_recv.at[place]).start()
 
+    def mix_pass(n):
+        return rcopy(mixrecv.at[n], mixrecv.at[n], mf_send.at[n], m_recv.at[n], sibling)
+
     value = acc[:, 256:512] * inv
-    vact = conv(jnp.concatenate([hprev[:, 0:256], value], 0), 0, 4, 256)
-    gact = silu(acc[:, 0:256] * inv)
-    step = mtile + pack[13:14, 0:128]
+    vact = conv(jnp.concatenate([hprev[:, 0:256], value], 0), vk, vo[...])
+    row = lax.broadcasted_iota(jnp.int32, (1, 128), 1)
+
+    def heads_row(ref):
+        out = jnp.zeros((1, 128), F32)
+        for h in range(4):
+            out = jnp.where(row == 64 + h, ref[0:1, h : h + 1], out)
+        return out
+
+    step = mtile + heads_row(so)
     step = jnp.maximum(step, 0.0) + jnp.log1p(jnp.exp(-jnp.abs(step)))
-    run = -step * pack[14:15, 0:128]
+    run = -step * jnp.exp(heads_row(dlog))
     for sh in (1, 2, 4, 8, 16):
         z0 = jnp.zeros((sh * LP, 128), F32)
         run = run + jnp.concatenate([z0, run[: ROWS - sh * LP]], 0)
     run_t = run.T
     lane = lax.broadcasted_iota(jnp.int32, (ROWS, LANES), 1)
 
-    def spread(t):
-        out = jnp.broadcast_to(t[:, 67:68], (ROWS, LANES))
+    def spread(t, at=64):
+        out = jnp.broadcast_to(t[:, at + 3 : at + 4], (t.shape[0], LANES))
         for h in (2, 1, 0):
-            out = jnp.where(lane < 64 * h + 64, t[:, 64 + h : 65 + h], out)
+            out = jnp.where(
+                lane[0 : t.shape[0]] < 64 * h + 64, t[:, at + h : at + h + 1], out
+            )
         return out
 
-    sv = vact * spread(step)
-    for h in range(4):
-        inside = (lane >= 64 * h) & (lane < 64 * h + 64)
-        sv4[h * ROWS : (h + 1) * ROWS, :] = jnp.where(inside, sv, 0.0).astype(BF16)
-
-    @pl.loop(0, 8)
-    def _(n):
-        rcopy(mixsend, mixrecv.at[n], m_send.at[n], m_recv.at[n], sibling).wait_recv()
+    for n in (4, 6):
+        mix_pass(n + c).wait_recv()
+        mix_pass(n + c).start()
+    for n in (4, 6):
+        mix_pass(n + 1 - c).wait_recv()
 
     def assemble(first_slot, dst):
         for t in range(2):
@@ -370,28 +452,38 @@
                 low, pltpu.roll(a, 64, 1), b
             ).astype(BF16)
 
+    cmat = call.at[d]
     assemble(4, cmat)
-    ccopies = [
-        rcopy(cmat, cre.at[o - 1], c_send.at[o - 1], c_recv.at[o - 1], dom(o))
-        for o in (1, 2, 3)
-    ]
-    for copy in ccopies:
-        copy.start()
-    assemble(0, bmat)
-
-    gram = lax.dot_general(cmat[...], bmat[...], NT, preferred_element_type=F32)
-    gi = lax.broadcasted_iota(jnp.int32, (ROWS, ROWS), 0)
-    gj = lax.broadcasted_iota(jnp.int32, (ROWS, ROWS), 1)
-    keep = ((gi % LP) == (gj % LP)) & (gj <= gi)
-    for h in range(4):
-        diff = jnp.where(keep, run[:, 64 + h : 65 + h] - run_t[64 + h : 65 + h, :], -1e30)
-        m4[:, h * ROWS : (h + 1) * ROWS] = (gram * jnp.exp(diff)).astype(BF16)
-    inner = jnp.dot(m4[...], sv4[...], preferred_element_type=F32)
-
-    def reads(cref, e):
+    x0 = pl.multiple_of(c * HALF, HALF)
+    quarter = HALF // 2
+
+    def c_copy(idx, recv):
+        e = (d + ((3, 1, 2, 2)[idx] if recv else (0, 0, 3, 1)[idx])) % 4
+        rows = (
+            pl.ds(x0, HALF),
+            pl.ds(x0, HALF),
+            pl.ds(x0, quarter),
+            pl.ds(x0 + quarter, quarter),
+        )[idx]
+        ref = call.at[e, rows]
+        return rcopy(ref, ref, c_send.at[idx], c_recv.at[idx], dom((1, 3)[idx % 2]))
+
+    def c_pass(o, recv):
+        start = pl.multiple_of((1 - c) * HALF, HALF) if recv else x0
+        ref = call.at[(d + o) % 4, pl.ds(start, HALF)]
+        return rcopy(ref, ref, cs_send.at[o - 1], cs_recv.at[o - 1], sibling)
+
+    c_copy(0, False).start()
+    c_copy(1, False).start()
+    for n in (0, 2):
+        mix_pass(n + c).wait_recv()
+        mix_pass(n + c).start()
+
+    def reads(e):
+        mine = par[pl.ds(pl.multiple_of(e * LP, LP), LP), :]
+
         def part(n, u):
-            cval = cref[...].reshape(STEPS, LP, LANES)
-            mine = par[pl.ds(pl.multiple_of(e * LP, LP), LP), :]
+            cval = call[e].reshape(STEPS, LP, LANES)
             lhs = []
             for t in range(4):
                 q = (d * LP + n * 4 + t).astype(F32)
@@ -406,21 +498,67 @@
 
         return lax.fori_loop(0, 4, part, jnp.zeros((ROWS, LANES), F32))
 
-    ucopies = []
-    for o in (1, 3, 2):
-        ccopies[o - 1].wait_recv()
-        usend[o - 1] = reads(cre.at[o - 1], (d + 4 - o) % 4).astype(BF16)
-        ucopies.append(
-            rcopy(usend.at[o - 1], urecv.at[o - 1], u_send.at[o - 1], u_recv.at[o - 1], dom(4 - o))
-        )
-        ucopies[-1].start()
-    start_read = reads(cmat, d)
-    for copy in ucopies:
-        copy.wait_recv()
-    for o in range(3):
-        start_read = start_read + urecv[o].astype(F32)
-    total = inner + jnp.exp(spread(run)) * start_read + pack[5:6, :] * vact
-    total = total * gact
+    start_read = reads(d)
+    for idx, o in ((0, 3), (1, 1)):
+        c_copy(idx, True).wait_recv()
+        c_copy(2 + idx, False).start()
+        c_pass(o, False).start()
+    for n in (0, 2):
+        mix_pass(n + 1 - c).wait_recv()
+    assemble(0, bmat)
+    gram = lax.dot_general(cmat[...], bmat[...], NT, preferred_element_type=F32)
+    gact = silu(acc[:, 0:256] * inv)
+    c_copy(2, True).wait_recv()
+    c_copy(3, True).wait_recv()
+    c_pass(2, False).start()
+    c_pass(2, True).wait_recv()
+    ufar[...] = reads((d + 2) % 4).astype(BF16)
+
+    def u_half(top):
+        rows = pl.ds(0 if top else HALF, HALF)
+        n = 0 if top else 1
+        return rcopy(
+            ufar.at[rows], ufarr.at[rows], u_send.at[n], u_recv.at[n], dom(1 if top else 3)
+        )
+
+    def u_full(n):
+        return rcopy(
+            usend.at[n], urecv.at[n], u_send.at[2 + n], u_recv.at[2 + n], dom(1 + 2 * n)
+        )
+
+    u_half(True).start()
+    u_half(False).start()
+    c_pass(1, True).wait_recv()
+    a = reads((d + 1) % 4).astype(BF16)
+    u_half(True).wait_recv()
+    usend[0, 0:HALF] = a[0:HALF] + ufarr[0:HALF]
+    usend[0, HALF:ROWS] = a[HALF:ROWS]
+    u_full(0).start()
+    c_pass(3, True).wait_recv()
+    a = reads((d + 3) % 4).astype(BF16)
+    u_half(False).wait_recv()
+    usend[1, 0:HALF] = a[0:HALF]
+    usend[1, HALF:ROWS] = a[HALF:ROWS] + ufarr[HALF:ROWS]
+    u_full(1).start()
+
+    sv = vact * spread(step)
+    for h in range(4):
+        inside = (lane >= 64 * h) & (lane < 64 * h + 64)
+        sv4[h * ROWS : (h + 1) * ROWS, :] = jnp.where(inside, sv, 0.0).astype(BF16)
+    gi = lax.broadcasted_iota(jnp.int32, (ROWS, ROWS), 0)
+    gj = lax.broadcasted_iota(jnp.int32, (ROWS, ROWS), 1)
+    keep = ((gi % LP) == (gj % LP)) & (gj <= gi)
+    for h in range(4):
+        diff = jnp.where(keep, run[:, 64 + h : 65 + h] - run_t[64 + h : 65 + h, :], -1e30)
+        m4[:, h * ROWS : (h + 1) * ROWS] = (gram * jnp.exp(diff)).astype(BF16)
+    inner = jnp.dot(m4[...], sv4[...], preferred_element_type=F32)
+    inner = inner + spread(skip[...], 0) * vact
+    carry = spread(jnp.exp(run))
+    u_full(0).wait_recv()
+    u_full(1).wait_recv()
+    start_read = start_read + urecv[0].astype(F32) + urecv[1].astype(F32)
+    total = (inner + carry * start_read) * gact
+    scaled[...] = (total * ogain[...]).astype(BF16)
     sq = lax.dot_general(
         jnp.ones((8, LANES), F32),
         total * total,
@@ -439,6 +577,28 @@
 
     for o in range(1, 8):
         sq_copy(o).start()
+
+    loads[10].wait()
+
+    def terms(slot):
+        return jnp.dot(
+            scaled[...],
+            wout[:, pl.ds(pl.multiple_of(slot * 256, 256), 256)],
+            preferred_element_type=F32,
+        )
+
+    def sib_terms(n):
+        return rcopy(sbuf.at[n], rbuf.at[n], rs_send.at[n], rs_recv.at[n], sibling)
+
+    def give(i, k):
+        n = i * 4 + k
+        sbuf[n] = terms(slot_sib(i, k)).astype(BF16)
+        sib_terms(n).start()
+
+    @pl.loop(0, 4)
+    def _(t):
+        give(3 - t, 3)
+
     for o in range(1, 8):
         at = (place8 + 8 - o) % 8
         rcopy(sqs.at[at], sqs.at[at], q_send.at[o - 1], q_recv.at[o - 1], sibling).wait_recv()
@@ -446,29 +606,11 @@
     for o in range(1, 8):
         tsq = tsq + sqs[o]
     inv2 = lax.rsqrt(tsq.T[:, 0:1] / 2048.0 + 1e-5)
-    scaled[...] = (total * inv2 * pack[6:7, :]).astype(BF16)
-
-    loads[10].wait()
-
-    def terms(slot):
-        return jnp.dot(
-            scaled[...],
-            wout[:, pl.ds(pl.multiple_of(slot * 256, 256), 256)],
-            preferred_element_type=F32,
-        )
-
-    def sib_terms(n):
-        return rcopy(sbuf.at[n], rbuf.at[n], rs_send.at[n], rs_recv.at[n], sibling)
-
-    @pl.loop(0, 16)
-    def _(t):
-        n = (3 - t % 4) * 4 + 3 - t // 4
-        sbuf[n] = terms(slot_sib(n // 4, n % 4)).astype(BF16)
-        sib_terms(n).start()
+    inv2s[...] = jnp.broadcast_to(inv2, (ROWS, LANES))
 
     def mine(i, k):
         sib_terms(i * 4 + k).wait_recv()
-        return terms(slot_own(i, k)) + rbuf[i * 4 + k].astype(F32)
+        return (terms(slot_own(i, k)) + rbuf[i * 4 + k].astype(F32)) * inv2s[...]
 
     def half_copy(i, top, to):
         rows = pl.ds(0 if top else HALF, HALF)
@@ -483,6 +625,8 @@
     @pl.loop(0, 4)
     def _(t):
         i = 3 - t
+        give(i, 1)
+        give(i, 2)
         hsend[i] = mine(i, 3).astype(BF16)
         half_copy(i, True, next2).start()
         half_copy(i, False, prev2).start()
@@ -490,6 +634,7 @@
     @pl.loop(0, 4)
     def _(t):
         i = 3 - t
+        give(i, 0)
         a = mine(i, 1)
         half_copy(i, True, next2).wait_recv()
         fsend[2 * i, 0:HALF] = (a[0:HALF] + hrecv[i, 0:HALF].astype(F32)).astype(BF16)
@@ -541,14 +686,21 @@
         to_sib(n // 4, n % 4).wait_send()
         sib_terms(n).wait_send()
 
-    @pl.loop(0, 8)
+    @pl.loop(0, 4)
     def _(n):
-        @pl.when(first + n != me)
+        @pl.when(first + 2 * n != me)
         def _():
             mix_copy(n).wait_send()
 
-    for copy in ccopies + ucopies:
-        copy.wait_send()
+        mix_pass(2 * n + c).wait_send()
+
+    for idx in range(4):
+        c_copy(idx, False).wait_send()
+    for o in (1, 2, 3):
+        c_pass(o, False).wait_send()
+    for flag in (0, 1):
+        u_half(flag == 0).wait_send()
+        u_full(flag).wait_send()
     for o in range(1, 8):
         sq_copy(o).wait_send()
     for i in range(5):
@@ -579,44 +731,6 @@
     ogain,
     ow,
 ):
-    d = lax.axis_index("dom")
-
-    def wide(a, at=0):
-        a = a.reshape(-1, a.shape[-1])
-        return jnp.pad(a, ((0, 0), (at, 256 - at - a.shape[-1])))
-
-    pack = jnp.concatenate(
-        [
-            vk,
-            wide(vo),
-            jnp.repeat(skip, 64)[None],
-            wide(ogain),
-            wide(gain),
-            wide(mk),
-            wide(mo),
-            wide(so, 64),
-            wide(jnp.exp(dlog), 64),
-            jnp.zeros((1, 256), F32),
-        ],
-        0,
-    )
-    hist = jnp.concatenate(
-        [
-            jnp.moveaxis(vhist, 1, 0),
-            jnp.pad(jnp.moveaxis(mhist, 1, 0), ((0, 0), (0, 0), (0, 64))),
-        ],
-        2,
-    )
-    hist = hist.astype(BF16).reshape(48, 384)
-    own = lax.dynamic_slice_in_dim(parents, d * LP, LP)
-    a = jnp.arange(48)[:, None]
-    b = jnp.arange(192)[None, :]
-    hsel = (
-        (a // LP == (b // LP) % 3)
-        & (jnp.tile(own, 3)[:, None] == (b // 48) * LP + b % LP)
-    ).astype(BF16)
-    par = jnp.broadcast_to(parents.astype(F32)[:, None], (64, 256))
-    step_t = jnp.pad(sw.T, ((0, 12), (0, 0)))
     v = gvw.reshape(8192, 2, 2, 128).transpose(0, 2, 1, 3).reshape(32768, 128)
 
     vmem = pl.BlockSpec(memory_space=pltpu.VMEM)
@@ -626,9 +740,23 @@
     out = pl.pallas_call(
         kernel,
         out_shape=jax.ShapeDtypeStruct(big, BF16),
-        in_specs=[vmem] * 6 + [hbm] * 4,
+        in_specs=[hbm] * 18,
         out_specs=vmem,
         scratch_shapes=[
+            pltpu.VMEM((1, 64), jnp.int32),
+            pltpu.VMEM((48, 256), F32),
+            pltpu.VMEM((48, 64), F32),
+            pltpu.VMEM((1, 256), F32),
+            pltpu.VMEM((4, 256), F32),
+            pltpu.VMEM((1, 256), F32),
+            pltpu.VMEM((4, 64), F32),
+            pltpu.VMEM((1, 64), F32),
+            pltpu.VMEM((1, 4), F32),
+            pltpu.VMEM((1, 4), F32),
+            pltpu.VMEM((1, 4), F32),
+            pltpu.VMEM((1, 256), F32),
+            pltpu.VMEM((4, 8192), BF16),
+            pltpu.VMEM((64, LANES), F32),
             pltpu.VMEM((32, TROWS, LANES), BF16),
             pltpu.VMEM((32768, 128), BF16),
             pltpu.VMEM((8192, 512), BF16),
@@ -643,16 +771,16 @@
             pltpu.VMEM((HALF, 128), BF16),
             pltpu.VMEM((8, HALF, 128), BF16),
             pltpu.VMEM(big, BF16),
+            pltpu.VMEM((4, *big), BF16),
             pltpu.VMEM(big, BF16),
-            pltpu.VMEM((3, *big), BF16),
-            pltpu.VMEM((3, *big), BF16),
-            pltpu.VMEM((3, *big), BF16),
-            pltpu.VMEM((8, 128), F32),
+            pltpu.VMEM(big, BF16),
+            pltpu.VMEM((2, *big), BF16),
+            pltpu.VMEM((2, *big), BF16),
             pltpu.VMEM((4 * ROWS, LANES), BF16),
             pltpu.VMEM((ROWS, 4 * ROWS), BF16),
-            pltpu.VMEM((8, 128), F32),
             pltpu.VMEM((8, 8, ROWS), F32),
             pltpu.VMEM(big, BF16),
+            pltpu.VMEM(big, F32),
             pltpu.VMEM((16, *big), BF16),
             pltpu.VMEM((16, *big), BF16),
             pltpu.VMEM((5, *big), BF16),
@@ -661,18 +789,22 @@
             pltpu.VMEM((10, *big), BF16),
             pltpu.VMEM((4, *big), F32),
             dma((11,)),
+            dma((14,)),
             dma((5, 4)),
             dma((5, 4)),
             dma((16,)),
             dma((16,)),
             dma((3,)),
             dma((3,)),
+            dma((4,)),
             dma((8,)),
             dma((8,)),
+            dma((4,)),
+            dma((4,)),
             dma((3,)),
             dma((3,)),
-            dma((3,)),
-            dma((3,)),
+            dma((4,)),
+            dma((4,)),
             dma((7,)),
             dma((7,)),
             dma((5, 4)),
@@ -687,11 +819,19 @@
         ),
     )(
         tokens.reshape(ROWS, LANES),
-        pack,
-        hist,
-        hsel,
-        par,
-        step_t,
+        parents.reshape(1, 64),
+        vhist.transpose(1, 0, 2).reshape(48, LANES),
+        mhist.transpose(1, 0, 2).reshape(48, 64),
+        gain.reshape(1, LANES),
+        vk,
+        vo.reshape(1, LANES),
+        mk,
+        mo.reshape(1, 64),
+        so.reshape(1, 4),
+        dlog.reshape(1, 4),
+        skip.reshape(1, 4),
+        ogain.reshape(1, LANES),
+        sw.T,
         v,
         mw.T,
         ow,

time: 118 us -> 94.8 us (0.80)
  Pallas kernels: 104 us -> 92.3 us
  local copies, waits for them, and re-layouts: 10.3 us -> 1.62 us
  other arithmetic: 3.52 us -> 0 us
    pallas_call x1, Pallas kernels: 104 us -> 92.3 us  [body(): pl.pallas_call(kernel, out_shape=jax.ShapeDtypeStruct(big, BF16), in_spec...]
    pad x6 -> x0, local copies, waits for them, and re-layouts: 3.72 us -> none  [the longest x4 2.15 us: wide(): return jnp.pad(a, ((0, 0), (at, 256 - at - a.shape[-1])))]
    concatenate x1 -> x0, local copies, waits for them, and re-layouts: 1.95 us -> none  [body(): jnp.concatenate([vk, wide(vo), jnp.repeat(skip, 64)[None], wide(ogain), w...]
    broadcast_in_dim x3 -> x0, local copies, waits for them, and re-layouts: 1.43 us -> none  [the longest x1 0.73 us: body(): jnp.repeat(skip, 64)[None]]
    convert_element_type x2 -> x0, other arithmetic: 1.34 us -> none  [the longest x1 0.68 us: body(): hsel = ((a // LP == b // LP % 3) & (jnp.tile(own, 3)[:, None] == b // 48...]
where the time goes in v3:
time: 94.8 us; the launch traced here: 93.9 us
  Pallas kernels  92.3 us (97%)
  local copies, waits for them, and re-layouts  1.62 us (2%)
    pallas_call x1, Pallas kernels, body(): pl.pallas_call(kernel, out_shape=jax.ShapeDtypeStruct(big, BF16), in_spec...  92.3 us

profile of v3, /device:TPU:0, one launch (start us, length us, event | category | flops | bytes accessed | tf_op | source)
XLA Modules:
  0.0 93.9 jit_solution(12869200059671676466)
XLA Ops:
  0.0 92.3 %shard_map.172 = bf16[384,256]{1,0:T(8,128)(2,1)} custom-call(bf16[384,256]{1,0:T(8,128)(2,1)} %bitcast.28, s32[1,64]{1,0:T(1,128)} %bitcast.35, f32[48,256]{1,0:T(8,128)} %bitcast.30, f32[48,64]{1,0:T(8,128)} %bitcast.31, f32[1,256]{1,0:T(1,128)} %bitcast.32, f32[4,256]{1,0:T(4,128)} %vk_hbm.1, f32[1,256]{1,0:T(1,128)} %bitcast.33, f32[4,64]{1,0:T(4,128)} %mk_hbm.1, ...), custom_call_target="tpu_custom_call" | custom-call | tf_op jit(solution)/shard_map/pallas_call | solution.py:740
  92.3 1.6 %copy.21 = bf16[24,16,256]{2,1,0:T(8,128)(2,1)} copy(bf16[24,16,256]{2,1,0:T(8,128)(2,1)} %bitcast.27) | data formatting | bytes 393216

commit v4 on v3

--- a/solution.py
+++ b/solution.py
@@ -73,6 +73,7 @@
     par,
     tok,
     vraw,
+    vtmp,
     w,
     ms,
     wout,
@@ -206,22 +207,31 @@
     pl.semaphore_wait(barrier, 8)
 
     def ring(grp, idx, recv):
-        k = (2, 1, 3, 3)[idx] if recv else (0, 0, 2, 1)[idx]
+        k = (2, 2, 1, 1, 3, 3)[idx] if recv else (0, 0, 0, 0, 2, 1)[idx]
         slot = slot_own(k, 0) if grp == 4 else slot_own(grp, k)
-        rows = (pl.ds(0, TROWS), pl.ds(0, TROWS), pl.ds(0, THALF), pl.ds(THALF, TROWS - THALF))[idx]
+        rows = (pl.ds(0, THALF), pl.ds(THALF, TROWS - THALF))[idx % 2]
         to = (next1, prev1) if grp == 4 else (next2, prev2)
         ref = tok.at[slot, rows]
-        return rcopy(ref, ref, a_send.at[grp, idx], a_recv.at[grp, idx], to[idx % 2])
+        return rcopy(
+            ref, ref, a_send.at[grp, idx], a_recv.at[grp, idx], to[(0, 0, 1, 1, 0, 1)[idx]]
+        )
+
+    def begin(grp, *idxs):
+        for idx in idxs:
+            ring(grp, idx, False).start()
+
+    def got(grp, idx):
+        ring(grp, idx, True).wait_recv()
 
     def to_sib(i, k, recv=False):
         slot = slot_sib(i, k) if recv else slot_own(i, k)
         ref = tok.at[slot]
         return rcopy(ref, ref, as_send.at[i * 4 + k], as_recv.at[i * 4 + k], sibling)
 
-    ring(4, 0, False).start()
-    ring(4, 1, False).start()
-    ring(0, 0, False).start()
-    ring(0, 1, False).start()
+    begin(4, 0, 3)
+    begin(0, 0, 3)
+    begin(4, 1, 2)
+    begin(0, 1, 2)
     to_sib(0, 0).start()
 
     hcopies = [
@@ -245,48 +255,61 @@
         (64, LANES),
     )
 
-    ri = lax.broadcasted_iota(jnp.int32, (256, 256), 0)
-    ci = lax.broadcasted_iota(jnp.int32, (256, 256), 1)
-    perm = (ci == 4 * (ri % 64) + ri // 64).astype(F32).astype(BF16)
-
     def split(b, _):
-        v0 = pl.multiple_of(b * 512, 512)
-        pair = jnp.concatenate(
-            [vraw[pl.ds(v0, 256), :], vraw[pl.ds(v0 + 256, 256), :]], axis=1
-        )
-        res = jnp.dot(perm, pair, preferred_element_type=F32).astype(BF16)
-        k0 = pl.multiple_of(b * 128, 128)
-        for n in range(2):
+        for u in range(2):
+            v0 = pl.multiple_of((b * 2 + u) * 512, 512)
+            vtmp[u] = vraw[pl.ds(v0, 512), :].astype(F32)
+        for u in range(2):
+            k0 = pl.multiple_of((b * 2 + u) * 128, 128)
             for j in range(2):
                 for r in range(2):
-                    m = 64 * (2 * j + r)
                     lane = 256 * r + 128 * j
-                    w[pl.ds(k0 + 64 * n, 64), lane : lane + 128] = res[
-                        m : m + 64, 128 * n : 128 * n + 128
-                    ]
+                    w[pl.ds(k0, 128), lane : lane + 128] = vtmp[
+                        u, pl.ds(2 * j + r, 128, stride=4), :
+                    ].astype(BF16)
         return 0
 
     for i in range(4):
         loads[i].wait()
-    lax.fori_loop(0, 32, split, 0)
-
-    for idx, k in ((0, 2), (1, 1)):
-        ring(4, idx, True).wait_recv()
-        ring(4, 2 + idx, False).start()
-        ring(k, 0, False).start()
-        ring(k, 1, False).start()
-        to_sib(k, 0).start()
+    lax.fori_loop(0, 8, split, 0)
+    got(4, 0)
+    begin(4, 4)
+    begin(2, 0, 2)
+    got(4, 3)
+    begin(4, 5)
+    begin(1, 3, 1)
+    lax.fori_loop(8, 16, split, 0)
+    got(4, 1)
+    begin(2, 3, 1)
+    to_sib(2, 0).start()
+    got(4, 2)
+    begin(1, 0, 2)
+    to_sib(1, 0).start()
+
+    def pass_on(i):
+        got(i, 0)
+        begin(i, 4)
+        got(i, 3)
+        begin(i, 5)
+        got(i, 1)
+        to_sib(i, 2).start()
+        got(i, 2)
+        to_sib(i, 1).start()
+
+    def far(i):
+        got(i, 4)
+        got(i, 5)
+        to_sib(i, 3).start()
+
     for i in range(4, 8):
         loads[i].wait()
-    lax.fori_loop(32, 64, split, 0)
-    for idx, k in ((0, 2), (1, 1)):
-        ring(0, idx, True).wait_recv()
-        ring(0, 2 + idx, False).start()
-        to_sib(0, k).start()
-    ring(4, 2, True).wait_recv()
-    ring(4, 3, True).wait_recv()
-    ring(3, 0, False).start()
-    ring(3, 1, False).start()
+    lax.fori_loop(16, 24, split, 0)
+    pass_on(0)
+    lax.fori_loop(24, 32, split, 0)
+    got(4, 4)
+    begin(3, 0, 2)
+    got(4, 5)
+    begin(3, 3, 1)
     to_sib(3, 0).start()
 
     loads[8].wait()
@@ -324,17 +347,6 @@
         sbf[:, pl.ds(pl.multiple_of(q * 256, 256), 256)] = st[q].astype(BF16)
         return 0
 
-    def pass_on(i):
-        for idx, k in ((0, 2), (1, 1)):
-            ring(i, idx, True).wait_recv()
-            ring(i, 2 + idx, False).start()
-            to_sib(i, k).start()
-
-    def far(i):
-        ring(i, 2, True).wait_recv()
-        ring(i, 3, True).wait_recv()
-        to_sib(i, 3).start()
-
     batch(1, lambda b: (b, 0))
     pass_on(1)
     batch(1, lambda b: (b + 1, 0))
@@ -482,21 +494,15 @@
     def reads(e):
         mine = par[pl.ds(pl.multiple_of(e * LP, LP), LP), :]
 
-        def part(n, u):
-            cval = call[e].reshape(STEPS, LP, LANES)
-            lhs = []
-            for t in range(4):
-                q = (d * LP + n * 4 + t).astype(F32)
-                mask = jnp.where(mine == q, 1.0, 0.0).astype(BF16)
-                lhs.append((cval * mask[None]).reshape(ROWS, LANES))
-            return u + lax.dot_general(
-                jnp.concatenate(lhs, 1),
-                sbf[:, pl.ds(pl.multiple_of(n * 1024, 1024), 1024)],
-                NT,
-                preferred_element_type=F32,
-            )
-
-        return lax.fori_loop(0, 4, part, jnp.zeros((ROWS, LANES), F32))
+        cval = call[e].reshape(STEPS, LP, LANES)
+        lhs = []
+        for n in range(LP):
+            q = (d * LP + n).astype(F32)
+            mask = jnp.where(mine == q, 1.0, 0.0).astype(BF16)
+            lhs.append((cval * mask[None]).reshape(ROWS, LANES))
+        return lax.dot_general(
+            jnp.concatenate(lhs, 1), sbf[...], NT, preferred_element_type=F32
+        )
 
     start_read = reads(d)
     for idx, o in ((0, 3), (1, 1)):
@@ -521,25 +527,27 @@
             ufar.at[rows], ufarr.at[rows], u_send.at[n], u_recv.at[n], dom(1 if top else 3)
         )
 
-    def u_full(n):
+    def u_full(n, top):
+        rows = pl.ds(0 if top else HALF, HALF)
+        m = 2 + 2 * n + (0 if top else 1)
         return rcopy(
-            usend.at[n], urecv.at[n], u_send.at[2 + n], u_recv.at[2 + n], dom(1 + 2 * n)
+            usend.at[n, rows], urecv.at[n, rows], u_send.at[m], u_recv.at[m], dom(1 + 2 * n)
         )
 
     u_half(True).start()
     u_half(False).start()
     c_pass(1, True).wait_recv()
-    a = reads((d + 1) % 4).astype(BF16)
+    usend[0] = reads((d + 1) % 4).astype(BF16)
+    u_full(0, False).start()
+    c_pass(3, True).wait_recv()
+    usend[1] = reads((d + 3) % 4).astype(BF16)
+    u_full(1, True).start()
     u_half(True).wait_recv()
-    usend[0, 0:HALF] = a[0:HALF] + ufarr[0:HALF]
-    usend[0, HALF:ROWS] = a[HALF:ROWS]
-    u_full(0).start()
-    c_pass(3, True).wait_recv()
-    a = reads((d + 3) % 4).astype(BF16)
+    usend[0, 0:HALF] = usend[0, 0:HALF] + ufarr[0:HALF]
+    u_full(0, True).start()
     u_half(False).wait_recv()
-    usend[1, 0:HALF] = a[0:HALF]
-    usend[1, HALF:ROWS] = a[HALF:ROWS] + ufarr[HALF:ROWS]
-    u_full(1).start()
+    usend[1, HALF:ROWS] = usend[1, HALF:ROWS] + ufarr[HALF:ROWS]
+    u_full(1, False).start()
 
     sv = vact * spread(step)
     for h in range(4):
@@ -554,8 +562,9 @@
     inner = jnp.dot(m4[...], sv4[...], preferred_element_type=F32)
     inner = inner + spread(skip[...], 0) * vact
     carry = spread(jnp.exp(run))
-    u_full(0).wait_recv()
-    u_full(1).wait_recv()
+    for n in range(2):
+        for top in (True, False):
+            u_full(n, top).wait_recv()
     start_read = start_read + urecv[0].astype(F32) + urecv[1].astype(F32)
     total = (inner + carry * start_read) * gact
     scaled[...] = (total * ogain[...]).astype(BF16)
@@ -590,14 +599,19 @@
     def sib_terms(n):
         return rcopy(sbuf.at[n], rbuf.at[n], rs_send.at[n], rs_recv.at[n], sibling)
 
-    def give(i, k):
-        n = i * 4 + k
-        sbuf[n] = terms(slot_sib(i, k)).astype(BF16)
-        sib_terms(n).start()
+    def give(*blocks):
+        made = [terms(slot_sib(i, k)).astype(BF16) for i, k in blocks]
+        for (i, k), block in zip(blocks, made):
+            sbuf[i * 4 + k] = block
+        for i, k in blocks:
+            sib_terms(i * 4 + k).start()
+
+    give((3, 3), (2, 3))
+    give((1, 3), (0, 3))
 
     @pl.loop(0, 4)
     def _(t):
-        give(3 - t, 3)
+        give((3 - t, 1), (3 - t, 2))
 
     for o in range(1, 8):
         at = (place8 + 8 - o) % 8
@@ -608,9 +622,9 @@
     inv2 = lax.rsqrt(tsq.T[:, 0:1] / 2048.0 + 1e-5)
     inv2s[...] = jnp.broadcast_to(inv2, (ROWS, LANES))
 
-    def mine(i, k):
+    def finish(own, i, k):
         sib_terms(i * 4 + k).wait_recv()
-        return (terms(slot_own(i, k)) + rbuf[i * 4 + k].astype(F32)) * inv2s[...]
+        return (own + rbuf[i * 4 + k].astype(F32)) * inv2s[...]
 
     def half_copy(i, top, to):
         rows = pl.ds(0 if top else HALF, HALF)
@@ -625,22 +639,22 @@
     @pl.loop(0, 4)
     def _(t):
         i = 3 - t
-        give(i, 1)
-        give(i, 2)
-        hsend[i] = mine(i, 3).astype(BF16)
+        hsend[i] = finish(terms(slot_own(i, 3)), i, 3).astype(BF16)
         half_copy(i, True, next2).start()
         half_copy(i, False, prev2).start()
 
     @pl.loop(0, 4)
     def _(t):
         i = 3 - t
-        give(i, 0)
-        a = mine(i, 1)
+        a = terms(slot_own(i, 1))
+        b = terms(slot_own(i, 2))
+        give((i, 0),)
+        a = finish(a, i, 1)
         half_copy(i, True, next2).wait_recv()
         fsend[2 * i, 0:HALF] = (a[0:HALF] + hrecv[i, 0:HALF].astype(F32)).astype(BF16)
         fsend[2 * i, HALF:ROWS] = a[HALF:ROWS].astype(BF16)
         full_copy(i, 0, next2).start()
-        b = mine(i, 2)
+        b = finish(b, i, 2)
         half_copy(i, False, prev2).wait_recv()
         fsend[2 * i + 1, 0:HALF] = b[0:HALF].astype(BF16)
         fsend[2 * i + 1, HALF:ROWS] = (
@@ -651,34 +665,48 @@
     @pl.loop(0, 4)
     def _(t):
         i = 3 - t
-        a = mine(i, 0)
+        rsum[i] = finish(terms(slot_own(i, 0)), i, 0)
+
+    def column(i):
         full_copy(i, 0, next2).wait_recv()
         full_copy(i, 1, prev2).wait_recv()
-        a = a + frecv[2 * i].astype(F32) + frecv[2 * i + 1].astype(F32)
-        rsum[i] = a
-
-        @pl.when(i == 3)
-        def _():
-            hsend[4] = a.astype(BF16)
-            half_copy(4, True, next1).start()
-            half_copy(4, False, prev1).start()
-
+        return rsum[i] + frecv[2 * i].astype(F32) + frecv[2 * i + 1].astype(F32)
+
+    hsend[4] = column(3).astype(BF16)
+    half_copy(4, True, next1).start()
+    half_copy(4, False, prev1).start()
+
+    def last_copy(n, top):
+        rows = pl.ds(0 if top else HALF, HALF)
+        m = 2 + 2 * n + (0 if top else 1)
+        return rcopy(
+            fsend.at[8 + n, rows],
+            frecv.at[8 + n, rows],
+            r_send.at[4, m],
+            r_recv.at[4, m],
+            (next1, prev1)[n],
+        )
+
+    b = column(2)
+    fsend[9, 0:HALF] = b[0:HALF].astype(BF16)
+    last_copy(1, True).start()
+    a = column(1)
+    fsend[8, HALF:ROWS] = a[HALF:ROWS].astype(BF16)
+    last_copy(0, False).start()
     half_copy(4, True, next1).wait_recv()
-    fsend[8, 0:HALF] = (rsum[1, 0:HALF] + hrecv[4, 0:HALF].astype(F32)).astype(BF16)
-    fsend[8, HALF:ROWS] = rsum[1, HALF:ROWS].astype(BF16)
-    full_copy(4, 0, next1).start()
+    fsend[8, 0:HALF] = (a[0:HALF] + hrecv[4, 0:HALF].astype(F32)).astype(BF16)
+    last_copy(0, True).start()
     half_copy(4, False, prev1).wait_recv()
-    fsend[9, 0:HALF] = rsum[2, 0:HALF].astype(BF16)
-    fsend[9, HALF:ROWS] = (
-        rsum[2, HALF:ROWS] + hrecv[4, HALF:ROWS].astype(F32)
-    ).astype(BF16)
-    full_copy(4, 1, prev1).start()
-    full_copy(4, 0, next1).wait_recv()
-    full_copy(4, 1, prev1).wait_recv()
-    out_ref[...] = (rsum[0] + frecv[8].astype(F32) + frecv[9].astype(F32)).astype(BF16)
+    fsend[9, HALF:ROWS] = (b[HALF:ROWS] + hrecv[4, HALF:ROWS].astype(F32)).astype(BF16)
+    last_copy(1, False).start()
+    a = column(0)
+    for n in range(2):
+        for top in (True, False):
+            last_copy(n, top).wait_recv()
+    out_ref[...] = (a + frecv[8].astype(F32) + frecv[9].astype(F32)).astype(BF16)
 
     for grp in range(5):
-        for idx in range(4):
+        for idx in range(6):
             ring(grp, idx, False).wait_send()
 
     @pl.loop(0, 16)
@@ -700,15 +728,21 @@
         c_pass(o, False).wait_send()
     for flag in (0, 1):
         u_half(flag == 0).wait_send()
-        u_full(flag).wait_send()
+        u_full(flag, True).wait_send()
+        u_full(flag, False).wait_send()
     for o in range(1, 8):
         sq_copy(o).wait_send()
     for i in range(5):
         nxt, prv = (next1, prev1) if i == 4 else (next2, prev2)
         half_copy(i, True, nxt).wait_send()
         half_copy(i, False, prv).wait_send()
-        full_copy(i, 0, nxt).wait_send()
-        full_copy(i, 1, prv).wait_send()
+        if i == 4:
+            for n in range(2):
+                last_copy(n, True).wait_send()
+                last_copy(n, False).wait_send()
+        else:
+            full_copy(i, 0, nxt).wait_send()
+            full_copy(i, 1, prv).wait_send()
 
 
 def body(
@@ -759,6 +793,7 @@
             pltpu.VMEM((64, LANES), F32),
             pltpu.VMEM((32, TROWS, LANES), BF16),
             pltpu.VMEM((32768, 128), BF16),
+            pltpu.VMEM((2, 512, 128), F32),
             pltpu.VMEM((8192, 512), BF16),
             pltpu.VMEM((128, 8192), BF16),
             pltpu.VMEM((256, 8192), BF16),
@@ -790,8 +825,8 @@
             pltpu.VMEM((4, *big), F32),
             dma((11,)),
             dma((14,)),
-            dma((5, 4)),
-            dma((5, 4)),
+            dma((5, 6)),
+            dma((5, 6)),
             dma((16,)),
             dma((16,)),
             dma((3,)),
@@ -803,12 +838,12 @@
             dma((4,)),
             dma((3,)),
             dma((3,)),
-            dma((4,)),
-            dma((4,)),
+            dma((6,)),
+            dma((6,)),
             dma((7,)),
             dma((7,)),
-            dma((5, 4)),
-            dma((5, 4)),
+            dma((5, 6)),
+            dma((5, 6)),
             dma((16,)),
             dma((16,)),
         ],

time: 94.8 us -> 88.2 us (0.930)
  Pallas kernels: 92.3 us -> 85.3 us
    pallas_call x1, Pallas kernels: 92.3 us -> 85.3 us  [body(): pl.pallas_call(kernel, out_shape=jax.ShapeDtypeStruct(big, BF16), in_spec...]
where the time goes in v4:
time: 88.2 us; the launch traced here: 86.9 us
  Pallas kernels  85.3 us (97%)
  local copies, waits for them, and re-layouts  1.62 us (2%)
    pallas_call x1, Pallas kernels, body(): pl.pallas_call(kernel, out_shape=jax.ShapeDtypeStruct(big, BF16), in_spec...  85.3 us

profile of v4, /device:TPU:0, one launch (start us, length us, event | category | flops | bytes accessed | tf_op | source)
XLA Modules:
  0.0 86.9 jit_solution(13943900549245749332)
XLA Ops:
  0.0 85.3 %shard_map.172 = bf16[384,256]{1,0:T(8,128)(2,1)} custom-call(bf16[384,256]{1,0:T(8,128)(2,1)} %bitcast.28, s32[1,64]{1,0:T(1,128)} %bitcast.35, f32[48,256]{1,0:T(8,128)} %bitcast.30, f32[48,64]{1,0:T(8,128)} %bitcast.31, f32[1,256]{1,0:T(1,128)} %bitcast.32, f32[4,256]{1,0:T(4,128)} %vk_hbm.1, f32[1,256]{1,0:T(1,128)} %bitcast.33, f32[4,64]{1,0:T(4,128)} %mk_hbm.1, ...), custom_call_target="tpu_custom_call" | custom-call | tf_op jit(solution)/shard_map/pallas_call | solution.py:774
  85.3 1.6 %copy.21 = bf16[24,16,256]{2,1,0:T(8,128)(2,1)} copy(bf16[24,16,256]{2,1,0:T(8,128)(2,1)} %bitcast.27) | data formatting | bytes 393216

commit v5 on v4

--- a/solution.py
+++ b/solution.py
@@ -229,9 +229,7 @@
         return rcopy(ref, ref, as_send.at[i * 4 + k], as_recv.at[i * 4 + k], sibling)
 
     begin(4, 0, 3)
-    begin(0, 0, 3)
     begin(4, 1, 2)
-    begin(0, 1, 2)
     to_sib(0, 0).start()
 
     hcopies = [
@@ -271,6 +269,8 @@
 
     for i in range(4):
         loads[i].wait()
+    begin(0, 0, 3)
+    begin(0, 1, 2)
     lax.fori_loop(0, 8, split, 0)
     got(4, 0)
     begin(4, 4)
@@ -347,23 +347,50 @@
         sbf[:, pl.ds(pl.multiple_of(q * 256, 256), 256)] = st[q].astype(BF16)
         return 0
 
-    batch(1, lambda b: (b, 0))
-    pass_on(1)
-    batch(1, lambda b: (b + 1, 0))
-    pass_on(2)
+    def pairs(*blocks):
+        (i0, k0), n = blocks[0], len(blocks)
+        di, dk = (blocks[1][0] - i0, blocks[1][1] - k0) if n > 1 else (0, 0)
+        batch(n, lambda b: (i0 + di * b, k0 + dk * b))
+
+    pairs((0, 0), (1, 0))
+    got(1, 0)
+    begin(1, 4)
+    got(1, 3)
+    begin(1, 5)
+    pairs((0, 1), (0, 2))
+    got(2, 0)
+    begin(2, 4)
+    got(2, 3)
+    begin(2, 5)
+    got(1, 1)
+    to_sib(1, 2).start()
+    got(1, 2)
+    to_sib(1, 1).start()
+    pairs((2, 0), (3, 0))
+    got(2, 1)
+    to_sib(2, 2).start()
+    got(2, 2)
+    to_sib(2, 1).start()
+    far(0)
     loads[9].wait()
     lax.fori_loop(0, LP, cast, 0)
-    far(0)
-    batch(2, lambda b: (2 + b, 0))
-    pass_on(3)
-    batch(3, lambda b: (0, b + 1))
+    pairs((1, 1), (1, 2))
+    got(3, 0)
+    begin(3, 4)
+    got(3, 3)
+    begin(3, 5)
+    pairs((2, 1), (2, 2))
+    got(3, 1)
+    to_sib(3, 2).start()
+    got(3, 2)
+    to_sib(3, 1).start()
     far(1)
-    batch(2, lambda b: (1, b + 1))
+    pairs((0, 3),)
     far(2)
-    batch(3, lambda b: (1 + (b + 2) // 3, 3 * (1 - (b + 2) // 3) + b))
-    batch(3, lambda b: (2 + (b + 1) // 2, 3 * (1 - (b + 1) // 2) + b))
+    pairs((1, 3),)
+    pairs((3, 1), (3, 2))
     far(3)
-    batch(1, lambda b: (3 + b, 3))
+    pairs((2, 3), (3, 3))
 
     inv = lax.rsqrt(jnp.sum(ss[...], axis=1, keepdims=True) / 8192.0 + 1e-5)
 
@@ -509,17 +536,6 @@
         c_copy(idx, True).wait_recv()
         c_copy(2 + idx, False).start()
         c_pass(o, False).start()
-    for n in (0, 2):
-        mix_pass(n + 1 - c).wait_recv()
-    assemble(0, bmat)
-    gram = lax.dot_general(cmat[...], bmat[...], NT, preferred_element_type=F32)
-    gact = silu(acc[:, 0:256] * inv)
-    c_copy(2, True).wait_recv()
-    c_copy(3, True).wait_recv()
-    c_pass(2, False).start()
-    c_pass(2, True).wait_recv()
-    ufar[...] = reads((d + 2) % 4).astype(BF16)
-
     def u_half(top):
         rows = pl.ds(0 if top else HALF, HALF)
         n = 0 if top else 1
@@ -534,14 +550,24 @@
             usend.at[n, rows], urecv.at[n, rows], u_send.at[m], u_recv.at[m], dom(1 + 2 * n)
         )
 
-    u_half(True).start()
-    u_half(False).start()
     c_pass(1, True).wait_recv()
     usend[0] = reads((d + 1) % 4).astype(BF16)
     u_full(0, False).start()
     c_pass(3, True).wait_recv()
     usend[1] = reads((d + 3) % 4).astype(BF16)
     u_full(1, True).start()
+    c_copy(2, True).wait_recv()
+    c_copy(3, True).wait_recv()
+    c_pass(2, False).start()
+    gact = silu(acc[:, 0:256] * inv)
+    c_pass(2, True).wait_recv()
+    ufar[...] = reads((d + 2) % 4).astype(BF16)
+    u_half(True).start()
+    u_half(False).start()
+    for n in (0, 2):
+        mix_pass(n + 1 - c).wait_recv()
+    assemble(0, bmat)
+    gram = lax.dot_general(cmat[...], bmat[...], NT, preferred_element_type=F32)
     u_half(True).wait_recv()
     usend[0, 0:HALF] = usend[0, 0:HALF] + ufarr[0:HALF]
     u_full(0, True).start()
@@ -567,7 +593,6 @@
             u_full(n, top).wait_recv()
     start_read = start_read + urecv[0].astype(F32) + urecv[1].astype(F32)
     total = (inner + carry * start_read) * gact
-    scaled[...] = (total * ogain[...]).astype(BF16)
     sq = lax.dot_general(
         jnp.ones((8, LANES), F32),
         total * total,
@@ -586,6 +611,7 @@
 
     for o in range(1, 8):
         sq_copy(o).start()
+    scaled[...] = (total * ogain[...]).astype(BF16)
 
     loads[10].wait()
 
@@ -703,7 +729,7 @@
     for n in range(2):
         for top in (True, False):
             last_copy(n, top).wait_recv()
-    out_ref[...] = (a + frecv[8].astype(F32) + frecv[9].astype(F32)).astype(BF16)
+    out_ref[...] = a + frecv[8].astype(F32) + frecv[9].astype(F32)
 
     for grp in range(5):
         for idx in range(6):
@@ -773,7 +799,7 @@
     big = (ROWS, LANES)
     out = pl.pallas_call(
         kernel,
-        out_shape=jax.ShapeDtypeStruct(big, BF16),
+        out_shape=jax.ShapeDtypeStruct(big, F32),
         in_specs=[hbm] * 18,
         out_specs=vmem,
         scratch_shapes=[
@@ -872,7 +898,7 @@
         ow,
         state.reshape(LP, 256, 256),
     )
-    return out.reshape(STEPS, LP, LANES)
+    return out.astype(BF16).reshape(STEPS, LP, LANES)
 
 
 def solution(mesh):

time: 88.2 us -> 87.5 us (level)
  other arithmetic: 0 us -> 1.69 us
  local copies, waits for them, and re-layouts: 1.62 us -> 0 us
    convert_element_type x0 -> x1, other arithmetic: none -> 1.69 us  [body(): return out.astype(BF16).reshape(STEPS, LP, LANES)]
    unnamed x1 -> x0, local copies, waits for them, and re-layouts: 1.62 us -> none
where the time goes in v5:
time: 87.5 us; the launch traced here: 86.4 us
  Pallas kernels  84.7 us (97%)
  other arithmetic  1.69 us (2%)
    pallas_call x1, Pallas kernels, body(): pl.pallas_call(kernel, out_shape=jax.ShapeDtypeStruct(big, F32), in_specs...  84.7 us

profile of v5, /device:TPU:0, one launch (start us, length us, event | category | flops | bytes accessed | tf_op | source)
XLA Modules:
  0.0 86.4 jit_solution(5989703132516068896)
XLA Ops:
  0.0 84.7 %shard_map.172 = f32[384,256]{1,0:T(8,128)} custom-call(bf16[384,256]{1,0:T(8,128)(2,1)} %bitcast.27, s32[1,64]{1,0:T(1,128)} %bitcast.34, f32[48,256]{1,0:T(8,128)} %bitcast.29, f32[48,64]{1,0:T(8,128)} %bitcast.30, f32[1,256]{1,0:T(1,128)} %bitcast.31, f32[4,256]{1,0:T(4,128)} %vk_hbm.1, f32[1,256]{1,0:T(1,128)} %bitcast.32, f32[4,64]{1,0:T(4,128)} %mk_hbm.1, ...), custom_call_target="tpu_custom_call" | custom-call | tf_op jit(solution)/shard_map/pallas_call | solution.py:800
  84.7 1.7 %convert_element_type.3 = bf16[384,256]{1,0:T(8,128)(2,1)} convert(f32[384,256]{1,0:T(8,128)} %shard_map.172) | non-fusion elementwise | flops 98304 | bytes 589824 | tf_op jit(solution)/shard_map/convert_element_type | solution.py:901
